TPU v7x, 32 devices: a whole 2x2x4 slice. The times are simulated.
32 devices in a mesh: gz: 4 (over z), gy: 2 (over y), gx: 4 (over x, core).
Axes of the slice: x: 2, y: 2, z: 4, core: 2. Of those that a mesh axis runs over, the one named last changes fastest.
Arguments:
- ref_image: float32 [64, 128, 512], P('gz', 'gy', 'gx'), may hold values from -40 to 40
- deformed_image: float32 [64, 128, 512], P('gz', 'gy', 'gx'), may hold values from -40 to 40
- nodal_disp: int32 [3, 8, 10, 36], P(None, 'gz', 'gy', 'gx'), may hold values from -1024 to 1023, as said below
Outputs:
- update: float32 [3, 8, 10, 36], P(None, 'gz', 'gy', 'gx')
- cg_residual: float32 [3, 8, 10, 36], P(None, 'gz', 'gy', 'gx')
Inputs may be any that keep to these rules, and one draw needn't show every extreme that they name: `nodal_disp`: copies of a node held by neighbouring bricks are equal.
All inputs are finite; a program needn't handle non-finite values.
Results may differ from a plain program's by a relative error of at most 0.0003.
Values sent between devices are 32-bit elements; how exact they have to be, the bound alone decides.
A program may use at most 256 MiB of HBM per device.

v0:
```python
import jax
import jax.numpy as jnp
from jax import lax
from jax.sharding import PartitionSpec as P

ELEM = 16
CGSTEPS = 8


quantum = 64
damping = 0.5


def padded(block, sides, width):
    for axis, dim in sides:
        count = lax.axis_size(axis)
        forward = [(i, i + 1) for i in range(count - 1)]
        backward = [(target, source) for source, target in forward]
        low = lax.ppermute(
            lax.slice_in_dim(block, block.shape[dim] - width, None, axis=dim), axis, forward
        )
        high = lax.ppermute(lax.slice_in_dim(block, 0, width, axis=dim), axis, backward)
        block = jnp.concatenate([low, block, high], axis=dim)
    return block


def weights():
    position = (jnp.arange(ELEM, dtype=jnp.float32) + 0.5) / ELEM
    return jnp.stack([1.0 - position, position])


def corners(field):
    count_z, count_y, count_x = (field.shape[1] - 1, field.shape[2] - 1, field.shape[3] - 1)
    pieces = []
    for offset in range(8):
        along_z, along_y, along_x = (offset >> 2, offset >> 1 & 1, offset & 1)
        pieces.append(
            field[
                :,
                along_z : along_z + count_z,
                along_y : along_y + count_y,
                along_x : along_x + count_x,
            ]
        )
    return jnp.stack(pieces, axis=1).reshape((field.shape[0], 2, 2, 2, count_z, count_y, count_x))


def assemble(parts):
    total = 0.0
    for offset in range(8):
        along_z, along_y, along_x = (offset >> 2, offset >> 1 & 1, offset & 1)
        total = total + jnp.pad(
            parts[:, along_z, along_y, along_x],
            ((0, 0), (along_z, 1 - along_z), (along_y, 1 - along_y), (along_x, 1 - along_x)),
        )
    return total


def blocks(volume):
    lead = volume.shape[:-3]
    count_z, count_y, count_x = (
        volume.shape[-3] // ELEM,
        volume.shape[-2] // ELEM,
        volume.shape[-1] // ELEM,
    )
    shaped = volume.reshape(lead + (count_z, ELEM, count_y, ELEM, count_x, ELEM))
    number = len(lead)
    order = tuple(range(number)) + (
        number + 1,
        number + 3,
        number + 5,
        number,
        number + 2,
        number + 4,
    )
    return jnp.transpose(shaped, order).reshape(
        lead + (ELEM, ELEM, ELEM, count_z * count_y * count_x)
    )


def element_terms(ref_pad, deformed_pad, nodes):
    count_z, count_y, count_x = (nodes.shape[1] - 1, nodes.shape[2] - 1, nodes.shape[3] - 1)
    image = ref_pad[1:-1, 1:-1, 1:-1]
    gradient = jnp.stack(
        [
            0.5 * (ref_pad[2:, 1:-1, 1:-1] - ref_pad[:-2, 1:-1, 1:-1]),
            0.5 * (ref_pad[1:-1, 2:, 1:-1] - ref_pad[1:-1, :-2, 1:-1]),
            0.5 * (ref_pad[1:-1, 1:-1, 2:] - ref_pad[1:-1, 1:-1, :-2]),
        ]
    )
    summed = jnp.sum(corners(nodes).reshape((3, 8, count_z, count_y, count_x)), axis=1)
    whole = jnp.floor_divide(summed, 8 * quantum)
    fraction = (summed - whole * (8 * quantum)).astype(jnp.float32) / (8.0 * quantum)
    anchor_z = jnp.arange(count_z, dtype=jnp.int32) * ELEM
    anchor_y = jnp.arange(count_y, dtype=jnp.int32) * ELEM
    anchor_x = jnp.arange(count_x, dtype=jnp.int32) * ELEM
    start_z = (anchor_z[:, None, None] + whole[0] + ELEM).reshape(-1)
    start_y = (anchor_y[None, :, None] + whole[1] + ELEM).reshape(-1)
    start_x = (anchor_x[None, None, :] + whole[2] + ELEM).reshape(-1)

    def cutout(first, second, third):
        return lax.dynamic_slice(
            deformed_pad, (first, second, third), (ELEM + 1, ELEM + 1, ELEM + 1)
        )

    boxes = jax.vmap(cutout, out_axes=3)(start_z, start_y, start_x)
    shares = fraction.reshape((3, -1))
    warped = (1.0 - shares[0]) * boxes[:-1] + shares[0] * boxes[1:]
    warped = (1.0 - shares[1]) * warped[:, :-1] + shares[1] * warped[:, 1:]
    warped = (1.0 - shares[2]) * warped[:, :, :-1] + shares[2] * warped[:, :, 1:]
    mismatch = blocks(image) - warped
    slopes = blocks(gradient)
    shape_fn = weights()
    scale = 1.0 / ELEM**2
    rhs = (
        jnp.einsum(
            "cijkn,ai,bj,dk->cabdn",
            slopes * mismatch,
            shape_fn,
            shape_fn,
            shape_fn,
            precision=lax.Precision.HIGHEST,
        )
        * scale
    )
    squared_weights = jnp.stack(
        [shape_fn[0] * shape_fn[0], shape_fn[0] * shape_fn[1], shape_fn[1] * shape_fn[1]]
    )
    moment_list = []
    for first, second in ((0, 0), (0, 1), (0, 2), (1, 1), (1, 2), (2, 2)):
        moment_list.append(
            jnp.einsum(
                "ijkn,si,tj,uk->stun",
                slopes[first] * slopes[second],
                squared_weights,
                squared_weights,
                squared_weights,
                precision=lax.Precision.HIGHEST,
            )
            * scale
        )
    moments = jnp.stack(moment_list).reshape((6, 3, 3, 3, count_z, count_y, count_x))
    return (rhs.reshape((3, 2, 2, 2, count_z, count_y, count_x)), moments)


def expand_moments(moments):
    pair_index = jnp.array([[0, 1, 2], [1, 3, 4], [2, 4, 5]], dtype=jnp.int32)
    levels = jnp.array([[0, 1], [1, 2]], dtype=jnp.int32)
    expanded = jnp.take(moments, pair_index, axis=0)
    expanded = jnp.take(expanded, levels, axis=2)
    expanded = jnp.take(expanded, levels, axis=4)
    expanded = jnp.take(expanded, levels, axis=6)
    return jnp.transpose(expanded, (0, 1, 2, 4, 6, 3, 5, 7, 8, 9, 10))


def apply_local(hessian, field):
    values = corners(field)
    result = jnp.einsum(
        "cdabgpqrxyz,dpqrxyz->cabgxyz", hessian, values, precision=lax.Precision.HIGHEST
    )
    return assemble(result)


def globalize(gathered, groups):
    lead = gathered.shape[1:-3]
    count_z, count_y, count_x = gathered.shape[-3:]
    along_z, along_y, along_x = groups
    shaped = gathered.reshape((along_z, along_y, along_x) + lead + (count_z, count_y, count_x))
    number = len(lead)
    order = tuple(range(3, 3 + number)) + (0, 3 + number, 1, 4 + number, 2, 5 + number)
    return jnp.transpose(shaped, order).reshape(
        lead + (along_z * count_z, along_y * count_y, along_x * count_x)
    )


def per_device(ref_image, deformed_image, nodal_disp):
    ref_pad = padded(ref_image, (("gz", 0), ("gy", 1), ("gx", 2)), 1)
    deformed_pad = padded(deformed_image, (("gz", 0), ("gy", 1), ("gx", 2)), ELEM)
    rhs_parts, moments = element_terms(ref_pad, deformed_pad, nodal_disp)
    count_z, count_y, count_x = (
        nodal_disp.shape[1] - 1,
        nodal_disp.shape[2] - 1,
        nodal_disp.shape[3] - 1,
    )
    gathered_rhs, gathered_moments = (
        lax.all_gather(rhs_parts[None], ("gz", "gy", "gx"), axis=0, tiled=True),
        lax.all_gather(moments[None], ("gz", "gy", "gx"), axis=0, tiled=True),
    )
    groups = (lax.axis_size("gz"), lax.axis_size("gy"), lax.axis_size("gx"))
    rhs = assemble(globalize(gathered_rhs, groups))
    hessian = expand_moments(globalize(gathered_moments, groups))
    solution = jnp.zeros_like(rhs)
    residual, direction = (rhs, rhs)
    norm_now = jnp.sum(residual * residual)
    for step in range(CGSTEPS):
        image = apply_local(hessian, direction) + damping * direction
        alpha = norm_now / jnp.sum(direction * image)
        solution = solution + alpha * direction
        residual = residual - alpha * image
        norm_next = jnp.sum(residual * residual)
        direction = residual + norm_next / norm_now * direction
        norm_now = norm_next
    zero = jnp.zeros((), jnp.int32)
    anchor = (
        zero,
        lax.axis_index("gz") * count_z,
        lax.axis_index("gy") * count_y,
        lax.axis_index("gx") * count_x,
    )
    extent = (3, count_z + 1, count_y + 1, count_x + 1)
    mine_solution = lax.dynamic_slice(solution, anchor, extent)
    mine_residual = lax.dynamic_slice(residual, anchor, extent)
    return (float(quantum) * mine_solution, mine_residual)


def solution(mesh):
    in_specs = (P("gz", "gy", "gx"), P("gz", "gy", "gx"), P(None, "gz", "gy", "gx"))
    out_specs = (P(None, "gz", "gy", "gx"), P(None, "gz", "gy", "gx"))
    return jax.shard_map(
        per_device, mesh=mesh, in_specs=in_specs, out_specs=out_specs, check_vma=False
    )
```

profile of v0, /device:TPU:0, one launch (start us, length us, event | category | flops | bytes accessed | tf_op | source)
XLA Modules:
  0.0 656.6 jit_solution(7606271038071672571)
XLA Ops:
  0.6 5.7 collective-permute-start.6
  54.3 6.6 fusion.14
  68.1 11.9 %maximum_bitcast_fusion = f32[3,16,16,16,1,4,8]{3,6,2,5,1,4,0:T(8,128)} fusion(f32[1,1,16,4,16,8,16]{6,5,4,3,2,1,0:T(8,128)} %stack.272, f32[1,1,16,4,16,8,16]{6,5,4,3,2,1,0:T(8,128)} %stack.271, f32[1,1,16,4,16,8,16]{6,5,4,3,2,1,0:T(8,128)} %stack.270), kind=kLoop, calls=%fused_computation.6 | loop fusion | flops 786432 | bytes 3145728 | tf_op jit(solution)/shard_map/transpose | solution.py:76
  80.1 9.7 %slice_multiply_fusion.6 = (f32[1,16,16,16,1,4,8]{3,6,2,5,1,4,0:T(8,128)}, f32[1,16,16,16,1,4,8]{3,6,2,5,1,4,0:T(8,128)}, f32[1,16,16,16,1,4,8]{3,6,2,5,1,4,0:T(...) fusion(f32[3,16,16,16,1,4,8]{3,6,2,5,1,4,0:T(8,128)} %maximum_b, ...), kind=kLoop, calls=%fused_computation.33 | loop fusion | flops 786432 | bytes 4718592 | tf_op jit(solution)/shard_map/mul | solution.py:134
  104.6 7.8 %copy_bitcast_fusion.2 = (f32[16,16,16,32]{2,3,1,0:T(8,128)}, f32[16,16,16,32]{2,3,1,0:T(8,128)}) fusion(f32[1,16,16,16,1,4,8]{3,6,2,5,1,4,0:T(8,128)} %get-tuple-element.68, f32[1,16,16,16,1,4,8]{3,6,2,5,1,4,0:T(8,128)} %get-tuple-element.70), kind=kLoop, calls=%fused_computation.29 | loop fusion | bytes 2097152 | tf_op jit(solution)/shard_map/mul | solution.py:134
  122.1 7.8 %copy_bitcast_fusion = (f32[16,16,16,32]{2,3,1,0:T(8,128)}, f32[16,16,16,32]{2,3,1,0:T(8,128)}) fusion(f32[1,16,16,16,1,4,8]{3,6,2,5,1,4,0:T(8,128)} %get-tuple-element.67, f32[1,16,16,16,1,4,8]{3,6,2,5,1,4,0:T(8,128)} %get-tuple-element.69), kind=kLoop, calls=%fused_computation.27 | loop fusion | bytes 2097152 | tf_op jit(solution)/shard_map/mul | solution.py:134
  164.5 5.3 collective-permute-start.10
  169.8 124.8 %all_gather.7 = f32[32,6,3,3,3,1,4,8]{7,6,5,4,3,2,1,0:T(4,128)S(1)} all-gather(f32[1,6,3,3,3,1,4,8]{7,6,5,4,3,2,1,0:T(4,128)} %constant_dynamic-update-slice_fusion.14), channel_id=1, replica_groups=mesh['gz'=4,'gy'=2,'gx'=4] {'gz','gy','gx'}, dimensions={0}, use_global_device_ids=true | all-gather | bytes 684288 | tf_op jit(solution)/shard_map/all_gather | solution.py:187
  294.6 6.0 copy.315
  300.7 10.2 %copy.316 = f32[6,3,3,3,4,1,2,4,4,8]{9,8,7,6,4,3,2,1,0,5:T(4,128)} copy(f32[6,3,3,3,4,1,2,4,4,8]{9,8,6,4,7,3,2,1,0,5:T(4,128)} %bitcast.593) | data formatting | bytes 1327104 | tf_op jit(solution)/shard_map/transpose | solution.py:171
  310.8 7.9 %reshape.335 = f32[6,3,3,3,4,8,32]{6,5,4,3,2,1,0:T(8,128)S(1)} reshape(f32[6,3,3,3,4,1,2,4,4,8]{9,8,7,6,4,3,2,1,0,5:T(4,128)} %copy.316) | data formatting | bytes 1327104 | tf_op jit(solution)/shard_map/reshape | solution.py:171
  321.4 5.3 gather_fusion.1
  326.8 6.4 gather_fusion.2
  333.2 7.7 %gather_fusion.3 = f32[4,3,3,2,2,2,2,4,8,32]{9,8,7,2,1,4,3,6,5,0:T(8,128)} fusion(f32[3,3,2,2,2,2,3,4,8,32]{9,8,7,6,1,0,3,2,5,4:T(8,128)} %bitcast.594, s32[1024]{0:T(1024)S(1)} %get-tuple-element.175), kind=kCustom, calls=%fused_computation.3 | custom fusion | bytes 4718608 | tf_op jit(solution)/shard_map/jit(_take)/gather | solution.py:152
  347.3 6.0 pad_maximum_fusion
  353.3 140.0 %while.1 = (s32[]{:T(128)}, f32[48,96,160]{2,1,0:T(8,128)}, s32[32,3]{0,1:T(4,128)S(1)}, f32[32,17,17,17]{3,2,1,0:T(8,128)}, s32[]{:T(128)}) while((s32[]{:T(128)}, f32[48,96,160]{2,1,0:T(8,128)}, s32[32,3]{0,1:T(4,128)S(1)}, f32[32,17,17,17]{3,2,1,0:T(8,128)}, s32[]{:T(128)}) %tuple.132), condition=%wide.while_cond, body=%wide.while_body.sunk | while | flops 2 | bytes 419453 | solution.py:102
  493.3 6.3 fusion
  507.0 5.5 bitcast_multiply_fusion
  512.4 9.8 %copy.280 = f32[3,16,16,16,32]{4,1,3,2,0:T(8,128)} copy(f32[3,16,16,16,32]{3,4,2,1,0:T(8,128)} %bitcast_multiply_fusion) | data formatting | bytes 3145728 | tf_op jit(solution)/shard_map/mul | solution.py:118
  522.2 5.1 fusion.45
  528.7 47.3 %all_gather.6 = f32[32,3,2,2,2,1,4,8]{7,6,5,4,3,2,1,0:T(4,128)S(1)} all-gather(f32[1,3,2,2,2,1,4,8]{7,6,5,4,3,2,1,0:T(4,128)S(1)} %copy.283), channel_id=1, replica_groups=mesh['gz'=4,'gy'=2,'gx'=4] {'gz','gy','gx'}, dimensions={0}, use_global_device_ids=true | all-gather | bytes 101376 | tf_op jit(solution)/shard_map/all_gather | solution.py:186
  578.5 5.0 multiply_reduce_fusion.7
  588.4 5.0 multiply_reduce_fusion.6
  617.9 5.2 multiply_reduce_fusion.3
  (365 shorter events, 315.7 us)
Async XLA Ops:
  0.6 139.6 %collective-permute-start.6 = (f32[16,64,128]{2,1,0:T(8,128)}, f32[16,64,128]{2,1,0:T(8,128)}, u32[]{:S(2)}, u32[]{:S(2)}) collective-permute-start(f32[16,64,128]{2,1,0:T(8,128)} %param.6), channel_id=1, source_target_pairs={{0,8},{8,16},{16,24},{1,9},{9,17},{17,25},{2,10},{10,18},{18,26},{... | collective-permute-start | bytes 1572872 | tf_op jit(solution)/shard_map/ppermute | solution.py:19
  6.4 135.2 %collective-permute-start.7 = (f32[16,64,128]{2,1,0:T(8,128)}, f32[16,64,128]{2,1,0:T(8,128)}, u32[]{:S(2)}, u32[]{:S(2)}) collective-permute-start(f32[16,64,128]{2,1,0:T(8,128)} %param.6), channel_id=1, source_target_pairs={{8,0},{16,8},{24,16},{9,1},{17,9},{25,17},{10,2},{18,10},{26,18},{... | collective-permute-start | bytes 1572872 | tf_op jit(solution)/shard_map/ppermute | solution.py:22
  8.4 9.2 %collective-permute-start.1 = (f32[1,64,128]{2,1,0:T(8,128)S(1)}, f32[1,64,128]{2,1,0:T(8,128)S(1)}, u32[]{:S(2)}, u32[]{:S(2)}) collective-permute-start(f32[1,64,128]{2,1,0:T(8,128)S(1)} %get-tuple-element.87), channel_id=1, source_target_pairs={{0,8},{8,16},{16,24},{1,9},{9,17},{17,25},{2,10},{10,18},{18,26},{... | collective-permute-start | bytes 98312 | tf_op jit(solution)/shard_map/ppermute | solution.py:19
  13.0 9.6 %collective-permute-start = (f32[1,64,128]{2,1,0:T(8,128)S(1)}, f32[1,64,128]{2,1,0:T(8,128)S(1)}, u32[]{:S(2)}, u32[]{:S(2)}) collective-permute-start(f32[1,64,128]{2,1,0:T(8,128)S(1)} %get-tuple-element.86), channel_id=1, source_target_pairs={{8,0},{16,8},{24,16},{9,1},{17,9},{25,17},{10,2},{18,10},{26,18},{... | collective-permute-start | bytes 98312 | tf_op jit(solution)/shard_map/ppermute | solution.py:22
  24.2 17.8 %collective-permute-start.3 = (f32[18,1,128]{2,0,1:T(8,128)S(1)}, f32[18,1,128]{2,0,1:T(8,128)S(1)}, u32[]{:S(2)}, u32[]{:S(2)}) collective-permute-start(f32[18,1,128]{2,0,1:T(8,128)S(1)} %copy.386), channel_id=1, source_target_pairs={{0,4},{1,5},{2,6},{3,7},{8,12},{9,13},{10,14},{11,15},{16,20},{17,... | collective-permute-start | bytes 27656 | tf_op jit(solution)/shard_map/ppermute | solution.py:19
  27.6 15.0 %collective-permute-start.2 = (f32[18,1,128]{2,0,1:T(8,128)S(1)}, f32[18,1,128]{2,0,1:T(8,128)S(1)}, u32[]{:S(2)}, u32[]{:S(2)}) collective-permute-start(f32[18,1,128]{2,0,1:T(8,128)S(1)} %copy.385), channel_id=1, source_target_pairs={{4,0},{5,1},{6,2},{7,3},{12,8},{13,9},{14,10},{15,11},{20,16},{21,... | collective-permute-start | bytes 27656 | tf_op jit(solution)/shard_map/ppermute | solution.py:22
  43.2 3.9 copy-start.6
  43.2 3.9 copy-start.7
  44.1 10.1 %collective-permute-start.5 = (f32[18,66,1]{1,0,2:T(8,128)S(1)}, f32[18,66,1]{1,0,2:T(8,128)S(1)}, u32[]{:S(2)}, u32[]{:S(2)}) collective-permute-start(f32[18,66,1]{1,0,2:T(8,128)S(1)} %get-tuple-element.76), channel_id=1, source_target_pairs={{0,1},{1,2},{2,3},{4,5},{5,6},{6,7},{8,9},{9,10},{10,11},{12,13},{... | collective-permute-start | bytes 14264 | tf_op jit(solution)/shard_map/ppermute | solution.py:19
  45.4 8.8 %collective-permute-start.4 = (f32[18,66,1]{1,0,2:T(8,128)S(1)}, f32[18,66,1]{1,0,2:T(8,128)S(1)}, u32[]{:S(2)}, u32[]{:S(2)}) collective-permute-start(f32[18,66,1]{1,0,2:T(8,128)S(1)} %get-tuple-element.75), channel_id=1, source_target_pairs={{1,0},{2,1},{3,2},{5,4},{6,5},{7,6},{9,8},{10,9},{11,10},{13,12},{... | collective-permute-start | bytes 14264 | tf_op jit(solution)/shard_map/ppermute | solution.py:22
  60.8 4.3 copy-start.8
  134.6 6.9 %copy-start.9 = (f32[16,64,128]{2,1,0:T(8,128)S(1)}, f32[16,64,128]{2,1,0:T(8,128)}, u32[]{:S(2)}) copy-start(f32[16,64,128]{2,1,0:T(8,128)} %param.6) | copy-start | bytes 1572868
  140.2 2.5 copy-start.10
  142.6 13.5 %copy-start.4 = (f32[48,64,128]{2,1,0:T(8,128)}, f32[48,64,128]{2,1,0:T(8,128)S(1)}, u32[]{:S(2)}) copy-start(f32[48,64,128]{2,1,0:T(8,128)S(1)} %constant_dynamic-update-slice_fusion.3) | copy-start | bytes 4718596
  142.7 11.7 %collective-permute-start.9 = (f32[48,16,128]{2,1,0:T(8,128)S(1)}, f32[48,16,128]{2,1,0:T(8,128)S(1)}, u32[]{:S(2)}, u32[]{:S(2)}) collective-permute-start(f32[48,16,128]{2,1,0:T(8,128)S(1)} %get-tuple-element.80), channel_id=1, source_target_pairs={{4,0},{5,1},{6,2},{7,3},{12,8},{13,9},{14,10},{15,11},{20,16},{21,... | collective-permute-start | bytes 1179656 | tf_op jit(solution)/shard_map/ppermute | solution.py:22
  144.0 12.1 %collective-permute-start.8 = (f32[48,16,128]{2,1,0:T(8,128)S(1)}, f32[48,16,128]{2,1,0:T(8,128)S(1)}, u32[]{:S(2)}, u32[]{:S(2)}) collective-permute-start(f32[48,16,128]{2,1,0:T(8,128)S(1)} %get-tuple-element.79), channel_id=1, source_target_pairs={{0,4},{1,5},{2,6},{3,7},{8,12},{9,13},{10,14},{11,15},{16,20},{17,... | collective-permute-start | bytes 1179656 | tf_op jit(solution)/shard_map/ppermute | solution.py:19
  161.8 179.1 %collective-permute-start.11 = (f32[48,96,16]{1,2,0:T(8,128)}, f32[48,96,16]{1,2,0:T(8,128)}, u32[]{:S(2)}, u32[]{:S(2)}) collective-permute-start(f32[48,96,16]{1,2,0:T(8,128)} %copy.276), channel_id=1, source_target_pairs={{1,0},{2,1},{3,2},{5,4},{6,5},{7,6},{9,8},{10,9},{11,10},{13,12},{... | collective-permute-start | bytes 884744 | tf_op jit(solution)/shard_map/ppermute | solution.py:22
  164.5 179.7 %collective-permute-start.10 = (f32[48,96,16]{1,2,0:T(8,128)}, f32[48,96,16]{1,2,0:T(8,128)}, u32[]{:S(2)}, u32[]{:S(2)}) collective-permute-start(f32[48,96,16]{1,2,0:T(8,128)} %copy.275), channel_id=1, source_target_pairs={{0,1},{1,2},{2,3},{4,5},{5,6},{6,7},{8,9},{9,10},{10,11},{12,13},{... | collective-permute-start | bytes 884744 | tf_op jit(solution)/shard_map/ppermute | solution.py:19
  340.9 6.4 copy-start.5
  499.5 2.2 copy-start.3
  501.7 4.2 copy-start.2
  503.5 2.5 copy-start
  503.5 3.5 copy-start.1
where the time goes:
time: 664 us; the launch traced here: 657 us
  local copies, waits for them, and re-layouts  293 us (44%)
  blocking collectives  172 us (26%)
  other arithmetic  107 us (16%)
  starting transfers between devices  32.9 us (5%)
  between operations  22.3 us (3%)
  matrix products  17.4 us (3%)
  waiting for transfers between devices  11.7 us (2%)
    gather x96, local copies, waits for them, and re-layouts  140 us
    all_gather x1, blocking collectives, per_device(): lax.all_gather(moments[None], ('gz', 'gy', 'gx'), axis=0, tiled=True)  125 us
    all_gather x1, blocking collectives, per_device(): lax.all_gather(rhs_parts[None], ('gz', 'gy', 'gx'), axis=0, tiled=True)  47.3 us
    unnamed x9, other arithmetic  40.3 us
    mul x9, local copies, waits for them, and re-layouts, element_terms(): slopes[first] * slopes[second]  38.4 us
    ppermute x6, starting transfers between devices, padded(): lax.ppermute(lax.slice_in_dim(block, block.shape[dim] - width, None, axis...  24.9 us
  transfers between devices with their start and end apart: 12, of which 4 were waited for; matrix products, arithmetic and copies ran while one was open for 25% of the time, Pallas kernels for 0%

commit v1 on v0

v1 whole, which is shorter than its diff:
```python
import functools

import jax
import jax.numpy as jnp
import numpy as np
from jax import lax
from jax.experimental import pallas as pl
from jax.experimental.pallas import tpu as pltpu
from jax.sharding import PartitionSpec as P

ELEM = 16
CGSTEPS = 8
QUANTUM = 64
DAMPING = 0.5
LANES = 128
SLOTS = LANES // ELEM
PAIRS = ((0, 0), (0, 1), (0, 2), (1, 1), (1, 2), (2, 2))
PAIR_OF = ((0, 1, 2), (1, 3, 4), (2, 4, 5))
GROUP = 14
GROUPS = 4

POSITION = (np.arange(ELEM) + 0.5) / ELEM
LINEAR = np.stack([1.0 - POSITION, POSITION])
SQUARED = np.stack([LINEAR[0] * LINEAR[0], LINEAR[0] * LINEAR[1], LINEAR[1] * LINEAR[1]])


def lane_of(shape):
    return lax.broadcasted_iota(jnp.int32, shape, len(shape) - 1)


def pack_face(load, first):
    rows = load(0).shape[0]
    slot = lane_of((rows, LANES)) // ELEM
    per = ELEM // SLOTS
    packed = []
    for part in range(per):
        total = load(part)
        total = pltpu.roll(total, (-first) % LANES, 1) if first else total
        for group in range(1, SLOTS):
            piece = pltpu.roll(load(group * per + part), (ELEM * group - first) % LANES, 1)
            total = jnp.where(slot == group, piece, total)
        packed.append(total)
    return packed


def pack_kernel(deformed_ref, ref_ref, to_low_ref, to_high_ref, ref_low_ref, ref_high_ref):
    for first, out, ref_out in ((0, to_low_ref, ref_low_ref), (LANES - ELEM, to_high_ref, ref_high_ref)):
        for brick in range(deformed_ref.shape[0] // ELEM):
            for part, value in enumerate(
                pack_face(lambda z, brick=brick: deformed_ref[brick * ELEM + z], first)
            ):
                out[brick, part] = value
        for part, value in enumerate(pack_face(lambda z: ref_ref[z], first)):
            ref_out[part] = value


def element_kernel(
    nodes_ref, wide_ref, from_low_ref, from_high_ref, image_ref, z_low_ref, z_high_ref,
    y_low_ref, y_high_ref, x_low_ref, x_high_ref, wy_ref, wx_ref, out_ref,
    low_ref, high_ref, ref_ref, warp_ref, u_ref,
):
    size_z, size_y, size_x = image_ref.shape
    count_y, count_x = size_y // ELEM, size_x // ELEM
    per = ELEM // SLOTS
    rows_wide = wide_ref.shape[1]
    lane_wide = lane_of((rows_wide, LANES))
    lane_y = lane_of((size_y, LANES))

    def spread(z, carry):
        brick, inner = z // ELEM, z % ELEM
        group, part = inner // per, inner % per
        centre = wide_ref[z]
        low = pltpu.roll(from_low_ref[brick, part], LANES - ELEM - ELEM * group, 1)
        low_ref[z] = jnp.where(lane_wide >= LANES - ELEM, low, centre)
        high = pltpu.roll(from_high_ref[brick, part], (LANES - ELEM * group) % LANES, 1)
        high_ref[z] = jnp.where(lane_wide < ELEM, high, centre)
        return carry

    lax.fori_loop(0, wide_ref.shape[0], spread, 0)

    ref_ref[0, 8 : 8 + size_y] = z_low_ref[...]
    ref_ref[size_z + 1, 8 : 8 + size_y] = z_high_ref[...]
    for z in range(size_z):
        ref_ref[z + 1, 0:8] = y_low_ref[z]
        ref_ref[z + 1, 8 : 8 + size_y] = image_ref[z]
        ref_ref[z + 1, 8 + size_y : 16 + size_y] = y_high_ref[z]

    u_ref[...] = jnp.zeros_like(u_ref)
    lane_16 = lane_of((ELEM, LANES))
    lane_8 = lane_of((8, LANES))

    def row(ey, carry):
        base = pl.multiple_of(ey * ELEM, ELEM)

        def element(source, ex):
            starts, shares = [], []
            for c in range(3):
                total = 0
                for offset in range(8):
                    total = total + nodes_ref[
                        c, offset >> 2, ey + (offset >> 1 & 1), ex + (offset & 1)
                    ]
                starts.append((total >> 9) + ELEM)
                shares.append((total & 511).astype(jnp.float32) * (1.0 / (8 * QUANTUM)))
            sz, sy, sx = starts
            fz, fy, fx = shares
            ys = base + sy
            back = (2 * LANES + ELEM - sx) % LANES
            back_next = (2 * LANES + ELEM - 1 - sx) % LANES
            mine = lane_16 // ELEM == ex

            def plane(z):
                return (1.0 - fy) * source[sz + z, pl.ds(ys, ELEM), :] + fy * source[
                    sz + z, pl.ds(ys + 1, ELEM), :
                ]

            before = plane(0)
            for z in range(ELEM):
                after = plane(z + 1)
                mixed = (1.0 - fz) * before + fz * after
                before = after
                value = (1.0 - fx) * pltpu.roll(mixed, back, 1) + fx * pltpu.roll(
                    mixed, back_next, 1
                )
                warp_ref[z] = jnp.where(mine, value, warp_ref[z])

        element(low_ref, 0)

        def middle(ex, carry):
            element(wide_ref, ex)
            return carry

        lax.fori_loop(1, count_x - 1, middle, 0)
        element(high_ref, count_x - 1)

        sums = []
        for half in range(ELEM // 8):
            squares = [[None] * 3 for _ in PAIRS]
            loads = [[None] * 2 for _ in range(3)]
            top = base + 8 * half
            for z in range(ELEM):
                here = ref_ref[z + 1, pl.ds(pl.multiple_of(top + 8, 8), 8), :]
                group, part = z // per, z % per
                slopes = [
                    0.5
                    * (
                        ref_ref[z + 2, pl.ds(pl.multiple_of(top + 8, 8), 8), :]
                        - ref_ref[z, pl.ds(pl.multiple_of(top + 8, 8), 8), :]
                    ),
                    0.5
                    * (
                        ref_ref[z + 1, pl.ds(top + 9, 8), :] - ref_ref[z + 1, pl.ds(top + 7, 8), :]
                    ),
                ]
                at = pl.multiple_of(top, 8)
                left = jnp.where(
                    lane_8 == 0,
                    pltpu.roll(x_low_ref[part, pl.ds(at, 8), :], (LANES - ELEM * group - ELEM + 1) % LANES, 1),
                    pltpu.roll(here, 1, 1),
                )
                right = jnp.where(
                    lane_8 == LANES - 1,
                    pltpu.roll(x_high_ref[part, pl.ds(at, 8), :], (LANES - 1 - ELEM * group) % LANES, 1),
                    pltpu.roll(here, LANES - 1, 1),
                )
                slopes.append(0.5 * (right - left))
                mismatch = here - warp_ref[z, 8 * half : 8 * half + 8, :]
                for index, (c, d) in enumerate(PAIRS):
                    product = slopes[c] * slopes[d]
                    for s in range(3):
                        term = float(SQUARED[s, z]) * product
                        squares[index][s] = term if z == 0 else squares[index][s] + term
                for c in range(3):
                    product = slopes[c] * mismatch
                    for a in range(2):
                        term = float(LINEAR[a, z]) * product
                        loads[c][a] = term if z == 0 else loads[c][a] + term
            sums.append((squares, loads))
        for half in range(2):
            squares, loads = sums[half]
        for index in range(len(PAIRS)):
            for s in range(3):
                for t in range(3):
                    total = sum(
                        sums[half][0][index][s] * wy_ref[t, 8 * half : 8 * half + 8, :]
                        for half in range(2)
                    )
                    kind = index * 9 + s * 3 + t
                    u_ref[pl.ds(kind * count_y + ey, 1), :] = jnp.sum(total, axis=0, keepdims=True)
        for c in range(3):
            for a in range(2):
                for b in range(2):
                    total = sum(
                        sums[half][1][c][a] * wy_ref[3 + b, 8 * half : 8 * half + 8, :]
                        for half in range(2)
                    )
                    kind = GROUP * GROUPS + c * 4 + a * 2 + b
                    u_ref[pl.ds(kind * count_y + ey, 1), :] = jnp.sum(total, axis=0, keepdims=True)
        return carry

    lax.fori_loop(0, count_y, row, 0)

    rows = GROUP * count_y
    total = 0.0
    for group in range(GROUPS + 1):
        total = total + jnp.dot(
            u_ref[group * rows : (group + 1) * rows, :],
            wx_ref[group],
            precision=lax.Precision.HIGHEST,
            preferred_element_type=jnp.float32,
        )
    out_ref[...] = total


def cg_kernel(axes, gathered_ref, update_ref, residual_ref, m_ref, s_ref, r_ref, d_ref):
    count_x, count_y, rows = axes
    places, groups_y = gathered_ref.shape[0], gathered_ref.shape[1]
    total_y = groups_y * count_y
    elems_x = lax.axis_size("gx") * count_x
    shape = (total_y, LANES)
    lane = lane_of(shape)
    line = lax.broadcasted_iota(jnp.int32, shape, 0)
    slot = lane // count_x
    per = 8 // count_y

    def unpack(pair, carry):
        at = pl.multiple_of(pair * 8, 8)
        tiles = [
            [gathered_ref[j, iy, pl.ds(at, 8), :] for iy in range(groups_y)] for j in range(places)
        ]
        for half in range(per):
            values = [
                jnp.concatenate(
                    [tile[half * count_y : (half + 1) * count_y] for tile in tiles[j]], axis=0
                )
                for j in range(places)
            ]
            step = 1
            while step < places:
                bit = (slot // step) % 2 == 0
                fresh = list(values)
                for j in range(places):
                    if (j // step) % 2 == 0:
                        first, second = values[j], values[j + step]
                        fresh[j] = jnp.where(bit, first, pltpu.roll(second, step * count_x, 1))
                        fresh[j + step] = jnp.where(
                            bit, pltpu.roll(first, LANES - step * count_x, 1), second
                        )
                values = fresh
                step *= 2
            for high in range(places):
                m_ref[high * GROUP + pair * per + half] = values[high]
        return carry

    lax.fori_loop(0, GROUP // per, unpack, 0)

    edge = {
        2: (lane % elems_x == 0, lane % elems_x == elems_x - 1, 1, 1),
        1: (line == 0, line == total_y - 1, 1, 0),
        0: (lane < elems_x, lane >= LANES - elems_x, elems_x, 1),
    }
    corner_list = [(a, b, g) for a in range(2) for b in range(2) for g in range(2)]
    keys = [(c,) + k for c in range(3) for k in corner_list]
    position = {key: index for index, key in enumerate(keys)}
    one = jnp.ones(shape, jnp.float32)
    own = {}
    for corner in corner_list:
        mask = one
        for dim in range(3):
            if corner[dim]:
                mask = jnp.where(edge[dim][1], mask, 0.0)
        own[corner] = mask

    def assemble(parts):
        for dim in range(3):
            first, last, shift, axis = edge[dim]
            extent = shape[axis]
            fresh = {}
            for key in keys:
                if key[1 + dim] == 0:
                    other = key[: 1 + dim] + (1,) + key[2 + dim :]
                    low, high = parts[key], parts[other]
                    fresh[key] = low + jnp.where(first, 0.0, pltpu.roll(high, shift, axis))
                    fresh[other] = high + jnp.where(last, 0.0, pltpu.roll(low, extent - shift, axis))
            parts = fresh
        return parts

    def squares(parts):
        total = {}
        for corner in corner_list:
            total[corner] = sum(parts[(c,) + corner] * parts[(c,) + corner] for c in range(3))
        return sum(total[corner] * own[corner] for corner in corner_list)

    parts = {}
    for c, a, b, g in keys:
        parts[c, a, b, g] = m_ref[(3 * GROUPS + g) * GROUP + c * 4 + a * 2 + b]
    parts = assemble(parts)
    for key in keys:
        s_ref[position[key]] = jnp.zeros(shape, jnp.float32)
        r_ref[position[key]] = parts[key]
        d_ref[position[key]] = parts[key]

    def step(index, norm_now):
        d = {key: d_ref[position[key]] for key in keys}
        image = {key: None for key in keys}
        for p, (first, second) in enumerate(PAIRS):
            orders = ((first, second),) if first == second else ((first, second), (second, first))
            for s in range(3):
                for t in range(3):
                    for u in range(3):
                        kind = p * 9 + s * 3 + t
                        value = m_ref[((kind // GROUP) * 3 + u) * GROUP + kind % GROUP]
                        for c, e in orders:
                            for a, b, g in corner_list:
                                q = (s - a, t - b, u - g)
                                if min(q) < 0 or max(q) > 1:
                                    continue
                                term = value * d[(e,) + q]
                                key = (c, a, b, g)
                                image[key] = term if image[key] is None else image[key] + term
        dots = sum(image[key] * d[key] for key in keys) + DAMPING * squares(d)
        alpha = norm_now / jnp.sum(dots)
        image = assemble(image)
        residual = {}
        for key in keys:
            at = position[key]
            s_ref[at] = s_ref[at] + alpha * d[key]
            residual[key] = r_ref[at] - alpha * (image[key] + DAMPING * d[key])
            r_ref[at] = residual[key]
        norm_next = jnp.sum(squares(residual))
        beta = norm_next / norm_now
        for key in keys:
            d_ref[position[key]] = residual[key] + beta * d[key]
        return norm_next

    start = {key: r_ref[position[key]] for key in keys}
    lax.fori_loop(0, CGSTEPS, step, jnp.sum(squares(start)))

    place = lax.axis_index("gz") * lax.axis_size("gx") + lax.axis_index("gx")
    first_lane = place * count_x
    first_line = lax.axis_index("gy") * count_y
    last_lane = (first_lane + count_x) % LANES
    last_line = (first_line + count_y) % total_y
    for source, out, scale in ((s_ref, update_ref, float(QUANTUM)), (r_ref, residual_ref, 1.0)):
        for c in range(3):
            for a in range(2):
                merged = []
                for b in range(2):
                    merged.append(
                        jnp.where(
                            lane == last_lane,
                            pltpu.roll(source[position[c, a, b, 1]], 1, 1),
                            source[position[c, a, b, 0]],
                        )
                    )
                value = jnp.where(line == last_line, pltpu.roll(merged[1], 1, 0), merged[0])
                value = pltpu.roll(value, (LANES - first_lane) % LANES, 1)
                value = pltpu.roll(value, (total_y - first_line) % total_y, 0)
                out[c, a] = scale * value[: count_y + 1, : count_x + 1]


def shifted(block, axis):
    count = lax.axis_size(axis)
    return [(i, i + 1) for i in range(count - 1)], [(i + 1, i) for i in range(count - 1)]


def exchange(to_low, to_high, axis):
    forward, backward = shifted(None, axis)
    return lax.ppermute(to_high, axis, forward), lax.ppermute(to_low, axis, backward)


def x_weights(count_x):
    table = np.zeros((GROUPS + 1, LANES, LANES), np.float32)
    scale = 1.0 / ELEM**2
    for group in range(GROUPS):
        for u in range(3):
            for k in range(count_x):
                column = (group * 3 + u) * count_x + k
                table[group, k * ELEM : (k + 1) * ELEM, column] = SQUARED[u] * scale
    for d in range(2):
        for k in range(count_x):
            column = (3 * GROUPS + d) * count_x + k
            table[GROUPS, k * ELEM : (k + 1) * ELEM, column] = LINEAR[d] * scale
    return jnp.asarray(table)


def y_weights():
    table = np.concatenate([SQUARED, LINEAR]).astype(np.float32)
    return jnp.asarray(np.broadcast_to(table[:, :, None], table.shape + (LANES,)))


VMEM = pl.BlockSpec(memory_space=pltpu.VMEM)
SMEM = pl.BlockSpec(memory_space=pltpu.SMEM)
PARAMS = pltpu.CompilerParams(vmem_limit_bytes=48 * 2**20)


def per_device(ref_image, deformed_image, nodal_disp):
    size_z, size_y, size_x = ref_image.shape
    count_y, count_x = size_y // ELEM, size_x // ELEM
    f32 = jnp.float32
    z_low, z_high = exchange(ref_image[:1], ref_image[-1:], "gz")
    y_low, y_high = exchange(ref_image[:, :8], ref_image[:, -8:], "gy")
    below, above = exchange(deformed_image, deformed_image, "gz")
    tall = jnp.concatenate([below, deformed_image, above], axis=0)
    left, right = exchange(tall[:, :ELEM], tall[:, -ELEM:], "gy")
    wide = jnp.concatenate([left, tall, right], axis=1)
    bricks = wide.shape[0] // ELEM
    per = ELEM // SLOTS
    face = jax.ShapeDtypeStruct((bricks, per, wide.shape[1], LANES), f32)
    ref_face = jax.ShapeDtypeStruct((per, size_y, LANES), f32)
    to_low, to_high, ref_to_low, ref_to_high = pl.pallas_call(
        pack_kernel,
        out_shape=(face, face, ref_face, ref_face),
        in_specs=[VMEM] * 2,
        out_specs=[VMEM] * 4,
        compiler_params=PARAMS,
    )(wide, ref_image)
    from_low, from_high = exchange(to_low, to_high, "gx")
    x_low, x_high = exchange(ref_to_low, ref_to_high, "gx")
    block = pl.pallas_call(
        element_kernel,
        out_shape=jax.ShapeDtypeStruct((GROUP * count_y, LANES), f32),
        in_specs=[SMEM] + [VMEM] * 12,
        out_specs=VMEM,
        scratch_shapes=[
            pltpu.VMEM(wide.shape, f32),
            pltpu.VMEM(wide.shape, f32),
            pltpu.VMEM((size_z + 2, size_y + 16, LANES), f32),
            pltpu.VMEM((ELEM, ELEM, LANES), f32),
            pltpu.VMEM((GROUP * (GROUPS + 1) * count_y, LANES), f32),
        ],
        compiler_params=PARAMS,
    )(
        nodal_disp, wide, from_low, from_high, ref_image, z_low[0], z_high[0],
        y_low, y_high, x_low, x_high, y_weights(), x_weights(count_x),
    )
    gathered = lax.all_gather(block, ("gz", "gx", "gy"), axis=0)
    groups = lax.axis_size("gz") * lax.axis_size("gx")
    gathered = gathered.reshape((groups, lax.axis_size("gy")) + block.shape)
    total_y = lax.axis_size("gy") * count_y
    fields = pltpu.VMEM((24, total_y, LANES), f32)
    nodes_out = jax.ShapeDtypeStruct(nodal_disp.shape, f32)
    return pl.pallas_call(
        functools.partial(cg_kernel, (count_x, count_y, block.shape[0])),
        out_shape=(nodes_out, nodes_out),
        in_specs=[VMEM],
        out_specs=[VMEM] * 2,
        scratch_shapes=[pltpu.VMEM((groups * GROUP, total_y, LANES), f32), fields, fields, fields],
        compiler_params=PARAMS,
    )(gathered)


def solution(mesh):
    in_specs = (P("gz", "gy", "gx"), P("gz", "gy", "gx"), P(None, "gz", "gy", "gx"))
    out_specs = (P(None, "gz", "gy", "gx"), P(None, "gz", "gy", "gx"))
    return jax.shard_map(
        per_device, mesh=mesh, in_specs=in_specs, out_specs=out_specs, check_vma=False
    )
```

time: 664 us -> 150 us (0.23); the launches traced: 657 us -> 150 us
  local copies, waits for them, and re-layouts: 293 us -> 2.55 us
  other arithmetic: 107 us -> 0.23 us
  blocking collectives: 172 us -> 70 us
  between operations: 22.3 us -> 0.88 us
  Pallas kernels: 0 us -> 21.1 us
  matrix products: 17.4 us -> 0 us
  waiting for transfers between devices: 11.7 us -> 25.8 us
    gather x100 -> x0, local copies, waits for them, and re-layouts: 162 us -> none
    all_gather x2 -> x1, blocking collectives: 172 us -> 70 us  [per_device(): gathered = lax.all_gather(block, ('gz', 'gx', 'gy'), axis=0)]
    mul x13 -> x0, local copies, waits for them, and re-layouts: 52.8 us -> none  [the longest x9 38.4 us: element_terms(): slopes[first] * slopes[second]]
    unnamed x9 -> x0, other arithmetic: 40.3 us -> none
    mul x10 -> x0, other arithmetic: 23.7 us -> none  [the longest x1 9.71 us: element_terms(): slopes[first] * slopes[second]]
    pallas_call x0 -> x3, Pallas kernels: none -> 21.1 us  [the longest x1 12.8 us: per_device(): pl.pallas_call(element_kernel, out_shape=jax.ShapeDtypeStruct((GROUP * co...]
    dot_general x21 -> x0, matrix products: 17.4 us -> none  [the longest x18 11.1 us: element_terms(): jnp.einsum('ijkn,si,tj,uk->stun', slopes[first] * slopes[second], squared...]
    reshape x4 -> x0, local copies, waits for them, and re-layouts: 17.4 us -> none  [the longest x2 8.69 us: globalize(): jnp.transpose(shaped, order)]
  transfers between devices with their start and end apart: 12 -> 12, of which waited for: 4 -> 7; matrix products, arithmetic and copies ran while one was open for 25% -> 1% of each run, Pallas kernels for 0% -> 1%
where the time goes in v1:
time: 150 us
  blocking collectives  70 us (47%)
  starting transfers between devices  29.1 us (19%)
  waiting for transfers between devices  25.8 us (17%)
  Pallas kernels  21.1 us (14%)
  local copies, waits for them, and re-layouts  2.55 us (2%)
    all_gather x1, blocking collectives, per_device(): gathered = lax.all_gather(block, ('gz', 'gx', 'gy'), axis=0)  70 us
    ppermute x6, starting transfers between devices, exchange(): lax.ppermute(to_high, axis, forward)  21.3 us
    ppermute x6, waiting for transfers between devices, exchange(): lax.ppermute(to_low, axis, backward)  13.5 us
    pallas_call x1, Pallas kernels, per_device(): pl.pallas_call(element_kernel, out_shape=jax.ShapeDtypeStruct((GROUP * co...  12.8 us
    ppermute x6, waiting for transfers between devices, exchange(): lax.ppermute(to_high, axis, forward)  12.4 us
    ppermute x6, starting transfers between devices, exchange(): lax.ppermute(to_low, axis, backward)  7.74 us
    pallas_call x1, Pallas kernels, per_device(): pl.pallas_call(functools.partial(cg_kernel, (count_x, count_y, block.shap...  6.93 us
  transfers between devices with their start and end apart: 12, of which 7 were waited for; matrix products, arithmetic and copies ran while one was open for 1% of the time, Pallas kernels for 1%

profile of v1, /device:TPU:0, one launch (start us, length us, event | category | flops | bytes accessed | tf_op | source)
XLA Modules:
  0.0 149.7 jit_solution(1613151254248482933)
XLA Ops:
  0.6 5.0 %collective-permute-start = (f32[16,64,128]{2,1,0:T(8,128)}, f32[16,64,128]{2,1,0:T(8,128)S(1)}, u32[]{:S(2)}, u32[]{:S(2)}) collective-permute-start(f32[16,64,128]{2,1,0:T(8,128)} %param.6), channel_id=1, source_target_pairs={{0,8},{8,16},{16,24},{1,9},{9,17},{17,25},{2,10},{10,18},{18,26},{... | collective-permute-start | bytes 1572872 | tf_op jit(solution)/shard_map/ppermute | solution.py:369
  5.6 1.3 collective-permute-start.1
  6.9 10.1 %collective-permute-done = f32[16,64,128]{2,1,0:T(8,128)S(1)} collective-permute-done((f32[16,64,128]{2,1,0:T(8,128)}, f32[16,64,128]{2,1,0:T(8,128)S(1)}, u32[]{:S(2)}, u32[]{:S(2)}) %collective-permute-start) | collective-permute-done | bytes 524320 | tf_op jit(solution)/shard_map/ppermute | solution.py:369
  17.1 1.1 constant_dynamic-update-slice_fusion.1
  18.2 2.9 %collective-permute-done.1 = f32[16,64,128]{2,1,0:T(8,128)S(1)} collective-permute-done((f32[16,64,128]{2,1,0:T(8,128)}, f32[16,64,128]{2,1,0:T(8,128)S(1)}, u32[]{:S(2)}, u32[]{:S(2)}) %collective-permute-start.1) | collective-permute-done | bytes 524320 | tf_op jit(solution)/shard_map/ppermute | solution.py:369
  21.2 3.4 %collective-permute-start.2 = (f32[48,16,128]{2,1,0:T(8,128)S(1)}, f32[48,16,128]{2,1,0:T(8,128)S(1)}, u32[]{:S(2)}, u32[]{:S(2)}) collective-permute-start(f32[48,16,128]{2,1,0:T(8,128)S(1)} %get-tuple-element.12), channel_id=1, source_target_pairs={{0,4},{1,5},{2,6},{3,7},{8,12},{9,13},{10,14},{11,15},{16,20},{17,... | collective-permute-start | bytes 1179656 | tf_op jit(solution)/shard_map/ppermute | solution.py:369
  24.6 1.3 collective-permute-start.3
  26.0 4.6 %collective-permute-start.8 = (f32[16,8,128]{2,1,0:T(8,128)S(1)}, f32[16,8,128]{2,1,0:T(8,128)S(1)}, u32[]{:S(2)}, u32[]{:S(2)}) collective-permute-start(f32[16,8,128]{2,1,0:T(8,128)S(1)} %get-tuple-element.15), channel_id=1, source_target_pairs={{0,4},{1,5},{2,6},{3,7},{8,12},{9,13},{10,14},{11,15},{16,20},{17,... | collective-permute-start | bytes 196616 | tf_op jit(solution)/shard_map/ppermute | solution.py:369
  30.6 1.9 %collective-permute-done.2 = f32[48,16,128]{2,1,0:T(8,128)S(1)} collective-permute-done((f32[48,16,128]{2,1,0:T(8,128)S(1)}, f32[48,16,128]{2,1,0:T(8,128)S(1)}, u32[]{:S(2)}, u32[]{:S(2)}) %collective-permute-start.2) | collective-permute-done | bytes 393248 | tf_op jit(solution)/shard_map/ppermute | solution.py:369
  32.5 3.4 %collective-permute-done.3 = f32[48,16,128]{2,1,0:T(8,128)S(1)} collective-permute-done((f32[48,16,128]{2,1,0:T(8,128)S(1)}, f32[48,16,128]{2,1,0:T(8,128)S(1)}, u32[]{:S(2)}, u32[]{:S(2)}) %collective-permute-start.3) | collective-permute-done | bytes 393248 | tf_op jit(solution)/shard_map/ppermute | solution.py:369
  36.2 1.4 shard_map.68
  37.6 1.3 collective-permute-start.4
  38.9 1.3 collective-permute-start.5
  40.2 3.5 %collective-permute-start.6 = (f32[1,64,128]{2,1,0:T(8,128)S(1)}, f32[1,64,128]{2,1,0:T(8,128)S(1)}, u32[]{:S(2)}, u32[]{:S(2)}) collective-permute-start(f32[1,64,128]{2,1,0:T(8,128)S(1)} %get-tuple-element.17), channel_id=1, source_target_pairs={{0,8},{8,16},{16,24},{1,9},{9,17},{17,25},{2,10},{10,18},{18,26},{... | collective-permute-start | bytes 98312 | tf_op jit(solution)/shard_map/ppermute | solution.py:369
  43.7 1.3 collective-permute-start.7
  45.3 1.3 collective-permute-start.9
  46.5 2.9 %collective-permute-done.7 = f32[1,64,128]{2,1,0:T(8,128)S(1)} collective-permute-done((f32[1,64,128]{2,1,0:T(8,128)S(1)}, f32[1,64,128]{2,1,0:T(8,128)S(1)}, u32[]{:S(2)}, u32[]{:S(2)}) %collective-permute-start.7) | collective-permute-done | bytes 32800 | tf_op jit(solution)/shard_map/ppermute | solution.py:369
  49.5 3.6 %collective-permute-start.10 = (f32[2,64,128]{2,1,0:T(8,128)S(1)}, f32[2,64,128]{2,1,0:T(8,128)S(1)}, u32[]{:S(2)}, u32[]{:S(2)}) collective-permute-start(f32[2,64,128]{2,1,0:T(8,128)S(1)} %get-tuple-element.8), channel_id=1, source_target_pairs={{0,1},{1,2},{2,3},{4,5},{5,6},{6,7},{8,9},{9,10},{10,11},{12,13},{... | collective-permute-start | bytes 196616 | tf_op jit(solution)/shard_map/ppermute | solution.py:369
  53.1 1.3 collective-permute-start.11
  54.4 4.2 %collective-permute-done.11.x_high_ref = f32[2,64,128]{2,1,0:T(8,128)S(1)} collective-permute-done((f32[2,64,128]{2,1,0:T(8,128)S(1)}, f32[2,64,128]{2,1,0:T(8,128)S(1)}, u32[]{:S(2)}, u32[]{:S(2)}) %collective-permute-start.11) | collective-permute-done | bytes 65568 | tf_op jit(solution)/shard_map/ppermute | solution.py:369
  58.7 12.8 %shard_map.69 = f32[56,128]{1,0:T(8,128)S(1)} custom-call(s32[3,2,5,9]{3,2,1,0:T(8,128)S(1)} %copy.7.nodes_ref, f32[48,96,128]{2,1,0:T(8,128)S(1)} %pad_maximum_fusion.deformed_ref.wide_ref, f32[3,2,96,128]{3,2,1,0:T(8,128)S(1)} %collective-permute-done.4.from_low_ref, f32[3,2,96,128]{3,2,1,0:T(8,128)S(1)} %collective-permute-done.5.from_high_ref, ...), custom_call_target="tpu_custom_call" | custom-call | tf_op jit(solution)/shard_map/pallas_call | solution.py:420
  71.5 70.0 %all-gather = f32[1792,128]{1,0:T(8,128)S(1)} all-gather(f32[56,128]{1,0:T(8,128)S(1)} %shard_map.69), channel_id=2, replica_groups=mesh['gz'=4,'gy'=2,'gx'=4] {'gz','gx','gy'}, dimensions={0}, use_global_device_ids=true | all-gather | bytes 946176 | tf_op jit(solution)/shard_map/all_gather | solution.py:437
  141.5 6.9 %shard_map.70 = (f32[3,2,5,9]{3,2,1,0:T(8,128)S(1)}, f32[3,2,5,9]{3,2,1,0:T(8,128)S(1)}) custom-call(f32[16,2,56,128]{3,2,1,0:T(8,128)S(1)} %bitcast.3), custom_call_target="tpu_custom_call" | custom-call | tf_op jit(solution)/shard_map/pallas_call | solution.py:443
  148.5 0.6 copy.8
  (23 shorter events, 1.4 us)
Async XLA Ops:
  0.6 16.4 %collective-permute-start = (f32[16,64,128]{2,1,0:T(8,128)}, f32[16,64,128]{2,1,0:T(8,128)S(1)}, u32[]{:S(2)}, u32[]{:S(2)}) collective-permute-start(f32[16,64,128]{2,1,0:T(8,128)} %param.6), channel_id=1, source_target_pairs={{0,8},{8,16},{16,24},{1,9},{9,17},{17,25},{2,10},{10,18},{18,26},{... | collective-permute-start | bytes 1572872 | tf_op jit(solution)/shard_map/ppermute | solution.py:369
  5.6 15.5 %collective-permute-start.1 = (f32[16,64,128]{2,1,0:T(8,128)}, f32[16,64,128]{2,1,0:T(8,128)S(1)}, u32[]{:S(2)}, u32[]{:S(2)}) collective-permute-start(f32[16,64,128]{2,1,0:T(8,128)} %param.6), channel_id=1, source_target_pairs={{8,0},{16,8},{24,16},{9,1},{17,9},{25,17},{10,2},{18,10},{26,18},{... | collective-permute-start | bytes 1572872 | tf_op jit(solution)/shard_map/ppermute | solution.py:369
  18.2 7.8 %copy-start = (f32[16,64,128]{2,1,0:T(8,128)S(1)}, f32[16,64,128]{2,1,0:T(8,128)}, u32[]{:S(2)}) copy-start(f32[16,64,128]{2,1,0:T(8,128)} %image_ref.1) | copy-start | bytes 1572868
  21.2 11.3 %collective-permute-start.2 = (f32[48,16,128]{2,1,0:T(8,128)S(1)}, f32[48,16,128]{2,1,0:T(8,128)S(1)}, u32[]{:S(2)}, u32[]{:S(2)}) collective-permute-start(f32[48,16,128]{2,1,0:T(8,128)S(1)} %get-tuple-element.12), channel_id=1, source_target_pairs={{0,4},{1,5},{2,6},{3,7},{8,12},{9,13},{10,14},{11,15},{16,20},{17,... | collective-permute-start | bytes 1179656 | tf_op jit(solution)/shard_map/ppermute | solution.py:369
  24.6 11.3 %collective-permute-start.3 = (f32[48,16,128]{2,1,0:T(8,128)S(1)}, f32[48,16,128]{2,1,0:T(8,128)S(1)}, u32[]{:S(2)}, u32[]{:S(2)}) collective-permute-start(f32[48,16,128]{2,1,0:T(8,128)S(1)} %get-tuple-element.13), channel_id=1, source_target_pairs={{4,0},{5,1},{6,2},{7,3},{12,8},{13,9},{14,10},{15,11},{20,16},{21,... | collective-permute-start | bytes 1179656 | tf_op jit(solution)/shard_map/ppermute | solution.py:369
  26.0 27.1 %collective-permute-start.8 = (f32[16,8,128]{2,1,0:T(8,128)S(1)}, f32[16,8,128]{2,1,0:T(8,128)S(1)}, u32[]{:S(2)}, u32[]{:S(2)}) collective-permute-start(f32[16,8,128]{2,1,0:T(8,128)S(1)} %get-tuple-element.15), channel_id=1, source_target_pairs={{0,4},{1,5},{2,6},{3,7},{8,12},{9,13},{10,14},{11,15},{16,20},{17,... | collective-permute-start | bytes 196616 | tf_op jit(solution)/shard_map/ppermute | solution.py:369
  36.2 18.2 %copy-start.2 = (s32[3,2,5,9]{3,1,2,0:T(2,128)S(1)}, s32[3,2,5,9]{3,1,2,0:T(2,128)}, u32[]{:S(2)}) copy-start(s32[3,2,5,9]{3,1,2,0:T(2,128)} %param.7) | copy-start | bytes 3244
  36.2 22.5 %copy-start.3 = (f32[5,16]{1,0:T(8,128)S(1)}, f32[5,16]{1,0:T(8,128)}, u32[]{:S(2)}) copy-start(f32[5,16]{1,0:T(8,128)} %constant.4.clone) | copy-start | bytes 964
  36.2 22.5 %copy-start.1 = (f32[5,128,128]{2,1,0:T(8,128)S(1)}, f32[5,128,128]{2,1,0:T(8,128)}, u32[]{:S(2)}) copy-start(f32[5,128,128]{2,1,0:T(8,128)} %constant.5.clone.wx_ref) | copy-start | bytes 983044
  37.6 21.0 %collective-permute-start.4 = (f32[3,2,96,128]{3,2,1,0:T(8,128)S(1)}, f32[3,2,96,128]{3,2,1,0:T(8,128)S(1)}, u32[]{:S(2)}, u32[]{:S(2)}) collective-permute-start(f32[3,2,96,128]{3,2,1,0:T(8,128)S(1)} %get-tuple-element.6), channel_id=1, source_target_pairs={{0,1},{1,2},{2,3},{4,5},{5,6},{6,7},{8,9},{9,10},{10,11},{12,13},{... | collective-permute-start | bytes 884744 | tf_op jit(solution)/shard_map/ppermute | solution.py:369
  38.9 19.7 %collective-permute-start.5 = (f32[3,2,96,128]{3,2,1,0:T(8,128)S(1)}, f32[3,2,96,128]{3,2,1,0:T(8,128)S(1)}, u32[]{:S(2)}, u32[]{:S(2)}) collective-permute-start(f32[3,2,96,128]{3,2,1,0:T(8,128)S(1)} %get-tuple-element.7), channel_id=1, source_target_pairs={{1,0},{2,1},{3,2},{5,4},{6,5},{7,6},{9,8},{10,9},{11,10},{13,12},{... | collective-permute-start | bytes 884744 | tf_op jit(solution)/shard_map/ppermute | solution.py:369
  40.2 5.0 %collective-permute-start.6 = (f32[1,64,128]{2,1,0:T(8,128)S(1)}, f32[1,64,128]{2,1,0:T(8,128)S(1)}, u32[]{:S(2)}, u32[]{:S(2)}) collective-permute-start(f32[1,64,128]{2,1,0:T(8,128)S(1)} %get-tuple-element.17), channel_id=1, source_target_pairs={{0,8},{8,16},{16,24},{1,9},{9,17},{17,25},{2,10},{10,18},{18,26},{... | collective-permute-start | bytes 98312 | tf_op jit(solution)/shard_map/ppermute | solution.py:369
  43.7 5.8 %collective-permute-start.7 = (f32[1,64,128]{2,1,0:T(8,128)S(1)}, f32[1,64,128]{2,1,0:T(8,128)S(1)}, u32[]{:S(2)}, u32[]{:S(2)}) collective-permute-start(f32[1,64,128]{2,1,0:T(8,128)S(1)} %get-tuple-element.16), channel_id=1, source_target_pairs={{8,0},{16,8},{24,16},{9,1},{17,9},{25,17},{10,2},{18,10},{26,18},{... | collective-permute-start | bytes 98312 | tf_op jit(solution)/shard_map/ppermute | solution.py:369
  45.3 9.2 %collective-permute-start.9 = (f32[16,8,128]{2,1,0:T(8,128)S(1)}, f32[16,8,128]{2,1,0:T(8,128)S(1)}, u32[]{:S(2)}, u32[]{:S(2)}) collective-permute-start(f32[16,8,128]{2,1,0:T(8,128)S(1)} %get-tuple-element.14), channel_id=1, source_target_pairs={{4,0},{5,1},{6,2},{7,3},{12,8},{13,9},{14,10},{15,11},{20,16},{21,... | collective-permute-start | bytes 196616 | tf_op jit(solution)/shard_map/ppermute | solution.py:369
  49.5 5.0 %collective-permute-start.10 = (f32[2,64,128]{2,1,0:T(8,128)S(1)}, f32[2,64,128]{2,1,0:T(8,128)S(1)}, u32[]{:S(2)}, u32[]{:S(2)}) collective-permute-start(f32[2,64,128]{2,1,0:T(8,128)S(1)} %get-tuple-element.8), channel_id=1, source_target_pairs={{0,1},{1,2},{2,3},{4,5},{5,6},{6,7},{8,9},{9,10},{10,11},{12,13},{... | collective-permute-start | bytes 196616 | tf_op jit(solution)/shard_map/ppermute | solution.py:369
  53.1 5.5 %collective-permute-start.11 = (f32[2,64,128]{2,1,0:T(8,128)S(1)}, f32[2,64,128]{2,1,0:T(8,128)S(1)}, u32[]{:S(2)}, u32[]{:S(2)}) collective-permute-start(f32[2,64,128]{2,1,0:T(8,128)S(1)} %get-tuple-element.9), channel_id=1, source_target_pairs={{1,0},{2,1},{3,2},{5,4},{6,5},{7,6},{9,8},{10,9},{11,10},{13,12},{... | collective-permute-start | bytes 196616 | tf_op jit(solution)/shard_map/ppermute | solution.py:369

commit v2 on v1

--- a/solution.py
+++ b/solution.py
@@ -43,15 +43,222 @@
     return packed
 
 
-def pack_kernel(deformed_ref, ref_ref, to_low_ref, to_high_ref, ref_low_ref, ref_high_ref):
-    for first, out, ref_out in ((0, to_low_ref, ref_low_ref), (LANES - ELEM, to_high_ref, ref_high_ref)):
-        for brick in range(deformed_ref.shape[0] // ELEM):
-            for part, value in enumerate(
-                pack_face(lambda z, brick=brick: deformed_ref[brick * ELEM + z], first)
+MESH = pl.DeviceIdType.MESH
+
+
+def neighbour_barrier(sides):
+    barrier = pltpu.get_barrier_semaphore()
+    count = 0
+    for axis, delta, exists in sides:
+
+        @pl.when(exists)
+        def _(axis=axis, delta=delta):
+            pl.semaphore_signal(
+                barrier, inc=1, device_id={axis: lax.axis_index(axis) + delta}, device_id_type=MESH
+            )
+
+        count = count + exists.astype(jnp.int32)
+    pl.semaphore_wait(barrier, count)
+
+
+def halo_kernel(
+    image_ref, deformed_ref, wide_ref, from_low_ref, from_high_ref, z_low_ref, z_high_ref,
+    y_low_ref, y_high_ref, x_low_ref, x_high_ref,
+    to_low_ref, to_high_ref, ref_low_ref, ref_high_ref, send_sem, recv_sem,
+):
+    size_z, size_y, _ = image_ref.shape
+    per = ELEM // SLOTS
+    low, high = {}, {}
+    for axis in ("gz", "gy", "gx"):
+        low[axis] = lax.axis_index(axis) > 0
+        high[axis] = lax.axis_index(axis) < lax.axis_size(axis) - 1
+    sides = [(axis, -1, low[axis]) for axis in low] + [(axis, 1, high[axis]) for axis in high]
+    neighbour_barrier(sides)
+    copies = []
+
+    def send(axis, delta, source, target):
+        index = len(copies)
+        copy = pltpu.make_async_remote_copy(
+            src_ref=source,
+            dst_ref=target,
+            send_sem=send_sem.at[index],
+            recv_sem=recv_sem.at[index],
+            device_id={axis: lax.axis_index(axis) + delta},
+            device_id_type=MESH,
+        )
+        sends, receives = (high[axis], low[axis]) if delta > 0 else (low[axis], high[axis])
+        copies.append((copy, sends))
+
+        @pl.when(sends)
+        def _():
+            copy.start()
+
+        def arrive():
+            @pl.when(receives)
+            def _():
+                copy.wait_recv()
+
+        def blank(*refs):
+            @pl.when(jnp.logical_not(receives))
+            def _():
+                for ref in refs:
+                    ref[...] = jnp.zeros(ref.shape, ref.dtype)
+
+        arrive.blank = blank
+        return arrive
+
+    rows = pl.ds(ELEM, size_y)
+    below, above = pl.ds(0, ELEM), pl.ds(2 * ELEM, ELEM)
+    waits = {}
+    waits["z", 0] = send("gz", 1, deformed_ref, wide_ref.at[below, rows])
+    waits["z", 2] = send("gz", -1, deformed_ref, wide_ref.at[above, rows])
+    middle = pl.ds(ELEM, ELEM)
+    first_rows, last_rows = pl.ds(0, ELEM), pl.ds(size_y - ELEM, ELEM)
+    into_low, into_high = pl.ds(0, ELEM), pl.ds(ELEM + size_y, ELEM)
+    center = [
+        send("gy", 1, deformed_ref.at[:, last_rows], wide_ref.at[middle, into_low]),
+        send("gy", -1, deformed_ref.at[:, first_rows], wide_ref.at[middle, into_high]),
+    ]
+    for value, face in ((0, ref_low_ref), (LANES - ELEM, ref_high_ref)):
+        for part, packed in enumerate(pack_face(lambda z: image_ref[z], value)):
+            face[part] = packed
+    others = [
+        send("gx", 1, ref_high_ref, x_low_ref),
+        send("gx", -1, ref_low_ref, x_high_ref),
+        send("gz", 1, image_ref.at[size_z - 1], z_low_ref),
+        send("gz", -1, image_ref.at[0], z_high_ref),
+        send("gy", 1, image_ref.at[:, pl.ds(size_y - 8, 8)], y_low_ref),
+        send("gy", -1, image_ref.at[:, pl.ds(0, 8)], y_high_ref),
+    ]
+    for arrive, ref in zip(
+        others, (x_low_ref, x_high_ref, z_low_ref, z_high_ref, y_low_ref, y_high_ref)
+    ):
+        arrive.blank(ref)
+    waits["z", 0].blank(wide_ref.at[below, rows])
+    waits["z", 2].blank(wide_ref.at[above, rows])
+    wide_ref[middle, rows] = deformed_ref[...]
+
+    def x_faces(brick, arrivals):
+        depth = pl.ds(brick * ELEM, ELEM)
+        arrivals[0].blank(wide_ref.at[depth, into_low])
+        arrivals[1].blank(wide_ref.at[depth, into_high])
+        for arrive in arrivals:
+            arrive()
+        for first, face in ((0, to_low_ref), (LANES - ELEM, to_high_ref)):
+            for part, packed in enumerate(
+                pack_face(lambda z: wide_ref[brick * ELEM + z], first)
             ):
-                out[brick, part] = value
-        for part, value in enumerate(pack_face(lambda z: ref_ref[z], first)):
-            ref_out[part] = value
+                face[brick, part] = packed
+        pair = [
+            send("gx", 1, to_high_ref.at[brick], from_low_ref.at[brick]),
+            send("gx", -1, to_low_ref.at[brick], from_high_ref.at[brick]),
+        ]
+        pair[0].blank(from_low_ref.at[brick])
+        pair[1].blank(from_high_ref.at[brick])
+        return pair
+
+    final = x_faces(1, center)
+    pending = {}
+    for brick in (0, 2):
+        waits["z", brick]()
+        depth = pl.ds(brick * ELEM, ELEM)
+        pending[brick] = [
+            send("gy", 1, wide_ref.at[depth, pl.ds(size_y, ELEM)], wide_ref.at[depth, into_low]),
+            send("gy", -1, wide_ref.at[depth, pl.ds(ELEM, ELEM)], wide_ref.at[depth, into_high]),
+        ]
+    for brick in (0, 2):
+        final += x_faces(brick, pending[brick])
+    for arrive in others + final:
+        arrive()
+    for copy, sends in copies:
+
+        @pl.when(sends)
+        def _(copy=copy):
+            copy.wait_send()
+
+
+HALO_COPIES = 20
+
+
+def gather_kernel(block_ref, gathered_ref, send_sem, recv_sem):
+    size_x, size_y, size_z = gathered_ref.shape[:3]
+    ix, iy, iz = lax.axis_index("gx"), lax.axis_index("gy"), lax.axis_index("gz")
+
+    def flip(index, step):
+        return index + step - 2 * step * ((index // step) % 2)
+
+    steps = []
+    step = size_x // 2
+    while step:
+        steps.append(step)
+        step //= 2
+    peers = [{"gz": (iz + hop) % size_z} for hop in range(1, size_z)]
+    peers += [{"gy": (iy + hop) % size_y} for hop in range(1, size_y)]
+    peers += [{"gx": flip(ix, step)} for step in steps]
+    barrier = pltpu.get_barrier_semaphore()
+    for peer in peers:
+        pl.semaphore_signal(barrier, inc=1, device_id=peer, device_id_type=MESH)
+    gathered_ref[ix, iy, iz] = block_ref[...]
+    pl.semaphore_wait(barrier, len(peers))
+    used = [0]
+    sent = []
+
+    def send(source, arriving, peer):
+        index = used[0]
+        used[0] += 1
+
+        def copy(ref):
+            return pltpu.make_async_remote_copy(
+                src_ref=ref,
+                dst_ref=ref,
+                send_sem=send_sem.at[index],
+                recv_sem=recv_sem.at[index],
+                device_id=peer,
+                device_id_type=MESH,
+            )
+
+        outgoing = copy(source)
+        outgoing.start()
+        sent.append(outgoing)
+        return copy(arriving)
+
+    phase = []
+    for hop in range(1, size_z):
+        phase.append(
+            send(
+                gathered_ref.at[ix, iy, iz],
+                gathered_ref.at[ix, iy, (iz + size_z - hop) % size_z],
+                peers[hop - 1],
+            )
+        )
+    for copy in phase:
+        copy.wait_recv()
+    phase = []
+    for hop in range(1, size_y):
+        phase.append(
+            send(
+                gathered_ref.at[ix, iy],
+                gathered_ref.at[ix, (iy + size_y - hop) % size_y],
+                peers[size_z - 2 + hop],
+            )
+        )
+    for copy in phase:
+        copy.wait_recv()
+    held = [ix]
+    for number, step in enumerate(steps):
+        phase = [
+            send(
+                gathered_ref.at[own],
+                gathered_ref.at[flip(own, step)],
+                peers[size_z + size_y - 2 + number],
+            )
+            for own in held
+        ]
+        for copy in phase:
+            copy.wait_recv()
+        held += [flip(own, step) for own in held]
+    for copy in sent:
+        copy.wait_send()
 
 
 def element_kernel(
@@ -214,7 +421,8 @@
 
 def cg_kernel(axes, gathered_ref, update_ref, residual_ref, m_ref, s_ref, r_ref, d_ref):
     count_x, count_y, rows = axes
-    places, groups_y = gathered_ref.shape[0], gathered_ref.shape[1]
+    groups_x, groups_y, groups_z = gathered_ref.shape[:3]
+    places = groups_z * groups_x
     total_y = groups_y * count_y
     elems_x = lax.axis_size("gx") * count_x
     shape = (total_y, LANES)
@@ -226,7 +434,11 @@
     def unpack(pair, carry):
         at = pl.multiple_of(pair * 8, 8)
         tiles = [
-            [gathered_ref[j, iy, pl.ds(at, 8), :] for iy in range(groups_y)] for j in range(places)
+            [
+                gathered_ref[j % groups_x, iy, j // groups_x, pl.ds(at, 8), :]
+                for iy in range(groups_y)
+            ]
+            for j in range(places)
         ]
         for half in range(per):
             values = [
@@ -359,16 +571,6 @@
                 out[c, a] = scale * value[: count_y + 1, : count_x + 1]
 
 
-def shifted(block, axis):
-    count = lax.axis_size(axis)
-    return [(i, i + 1) for i in range(count - 1)], [(i + 1, i) for i in range(count - 1)]
-
-
-def exchange(to_low, to_high, axis):
-    forward, backward = shifted(None, axis)
-    return lax.ppermute(to_high, axis, forward), lax.ppermute(to_low, axis, backward)
-
-
 def x_weights(count_x):
     table = np.zeros((GROUPS + 1, LANES, LANES), np.float32)
     scale = 1.0 / ELEM**2
@@ -398,25 +600,30 @@
     size_z, size_y, size_x = ref_image.shape
     count_y, count_x = size_y // ELEM, size_x // ELEM
     f32 = jnp.float32
-    z_low, z_high = exchange(ref_image[:1], ref_image[-1:], "gz")
-    y_low, y_high = exchange(ref_image[:, :8], ref_image[:, -8:], "gy")
-    below, above = exchange(deformed_image, deformed_image, "gz")
-    tall = jnp.concatenate([below, deformed_image, above], axis=0)
-    left, right = exchange(tall[:, :ELEM], tall[:, -ELEM:], "gy")
-    wide = jnp.concatenate([left, tall, right], axis=1)
-    bricks = wide.shape[0] // ELEM
     per = ELEM // SLOTS
-    face = jax.ShapeDtypeStruct((bricks, per, wide.shape[1], LANES), f32)
+    wide = jax.ShapeDtypeStruct((3 * ELEM, size_y + 2 * ELEM, LANES), f32)
+    face = jax.ShapeDtypeStruct((3, per, size_y + 2 * ELEM, LANES), f32)
     ref_face = jax.ShapeDtypeStruct((per, size_y, LANES), f32)
-    to_low, to_high, ref_to_low, ref_to_high = pl.pallas_call(
-        pack_kernel,
-        out_shape=(face, face, ref_face, ref_face),
+    plane = jax.ShapeDtypeStruct((size_y, LANES), f32)
+    edge = jax.ShapeDtypeStruct((size_z, 8, LANES), f32)
+    halos = pl.pallas_call(
+        halo_kernel,
+        out_shape=(wide, face, face, plane, plane, edge, edge, ref_face, ref_face),
         in_specs=[VMEM] * 2,
-        out_specs=[VMEM] * 4,
-        compiler_params=PARAMS,
-    )(wide, ref_image)
-    from_low, from_high = exchange(to_low, to_high, "gx")
-    x_low, x_high = exchange(ref_to_low, ref_to_high, "gx")
+        out_specs=[VMEM] * 9,
+        scratch_shapes=[
+            pltpu.VMEM(face.shape, f32),
+            pltpu.VMEM(face.shape, f32),
+            pltpu.VMEM(ref_face.shape, f32),
+            pltpu.VMEM(ref_face.shape, f32),
+            pltpu.SemaphoreType.DMA((HALO_COPIES,)),
+            pltpu.SemaphoreType.DMA((HALO_COPIES,)),
+        ],
+        compiler_params=pltpu.CompilerParams(
+            vmem_limit_bytes=48 * 2**20, collective_id=0, has_side_effects=True
+        ),
+    )(ref_image, deformed_image)
+    wide, from_low, from_high, z_low, z_high, y_low, y_high, x_low, x_high = halos
     block = pl.pallas_call(
         element_kernel,
         out_shape=jax.ShapeDtypeStruct((GROUP * count_y, LANES), f32),
@@ -431,12 +638,22 @@
         ],
         compiler_params=PARAMS,
     )(
-        nodal_disp, wide, from_low, from_high, ref_image, z_low[0], z_high[0],
+        nodal_disp, wide, from_low, from_high, ref_image, z_low, z_high,
         y_low, y_high, x_low, x_high, y_weights(), x_weights(count_x),
     )
-    gathered = lax.all_gather(block, ("gz", "gx", "gy"), axis=0)
-    groups = lax.axis_size("gz") * lax.axis_size("gx")
-    gathered = gathered.reshape((groups, lax.axis_size("gy")) + block.shape)
+    sizes = tuple(lax.axis_size(axis) for axis in ("gx", "gy", "gz"))
+    groups = sizes[0] * sizes[2]
+    copies = sum(sizes) - 3 + sizes[0]
+    gathered = pl.pallas_call(
+        gather_kernel,
+        out_shape=jax.ShapeDtypeStruct(sizes + block.shape, f32),
+        in_specs=[VMEM],
+        out_specs=VMEM,
+        scratch_shapes=[pltpu.SemaphoreType.DMA((copies,)), pltpu.SemaphoreType.DMA((copies,))],
+        compiler_params=pltpu.CompilerParams(
+            vmem_limit_bytes=48 * 2**20, collective_id=1, has_side_effects=True
+        ),
+    )(block)
     total_y = lax.axis_size("gy") * count_y
     fields = pltpu.VMEM((24, total_y, LANES), f32)
     nodes_out = jax.ShapeDtypeStruct(nodal_disp.shape, f32)

time: 150 us -> 70.1 us (0.47)
  blocking collectives: 70 us -> 0 us
  Pallas kernels: 21.1 us -> 63.4 us
  starting transfers between devices: 29.1 us -> 0 us
  waiting for transfers between devices: 25.8 us -> 0 us
  local copies, waits for them, and re-layouts: 2.55 us -> 5.76 us
    all_gather x1 -> x0, blocking collectives: 70 us -> none  [per_device(): gathered = lax.all_gather(block, ('gz', 'gx', 'gy'), axis=0)]
    pallas_call x1 -> x2, Pallas kernels: 1.38 us -> 43.7 us  [the longest x1 23.2 us: per_device(): pl.pallas_call(halo_kernel, out_shape=(wide, face, face, plane, plane, ed...]
    ppermute x12 -> x0, starting transfers between devices: 29.1 us -> none  [the longest x6 21.3 us: exchange(): lax.ppermute(to_high, axis, forward)]
    ppermute x12 -> x0, waiting for transfers between devices: 25.8 us -> none  [the longest x6 13.5 us: exchange(): lax.ppermute(to_low, axis, backward)]
    unnamed x11 -> x7, local copies, waits for them, and re-layouts: 1.15 us -> 3.78 us
  transfers between devices with their start and end apart: 12 -> 0, of which waited for: 7 -> 0; matrix products, arithmetic and copies ran while one was open for 1% -> 0% of each run, Pallas kernels for 1% -> 0%
where the time goes in v2:
time: 70.1 us; the launch traced here: 69.8 us
  Pallas kernels  63.4 us (90%)
  local copies, waits for them, and re-layouts  5.76 us (8%)
    pallas_call x1, Pallas kernels, per_device(): pl.pallas_call(halo_kernel, out_shape=(wide, face, face, plane, plane, ed...  23.2 us
    pallas_call x1, Pallas kernels, per_device(): pl.pallas_call(gather_kernel, out_shape=jax.ShapeDtypeStruct(sizes + bloc...  20.4 us
    pallas_call x1, Pallas kernels, per_device(): pl.pallas_call(element_kernel, out_shape=jax.ShapeDtypeStruct((GROUP * co...  12.8 us
    pallas_call x1, Pallas kernels, per_device(): pl.pallas_call(functools.partial(cg_kernel, (count_x, count_y, block.shap...  6.94 us
    unnamed x7, local copies, waits for them, and re-layouts  3.78 us

profile of v2, /device:TPU:0, one launch (start us, length us, event | category | flops | bytes accessed | tf_op | source)
XLA Modules:
  0.0 69.8 jit_solution(10489344425910905590)
XLA Ops:
  0.6 0.7 %copy.7.nodes_ref = s32[3,2,5,9]{3,2,1,0:T(8,128)S(1)} copy(s32[3,2,5,9]{3,1,2,0:T(2,128)} %param.7) | data formatting | bytes 2160 | tf_op args[2]
  1.4 0.0 copy-start
  1.4 1.0 %copy-done = f32[16,64,128]{2,1,0:T(8,128)S(1)} copy-done((f32[16,64,128]{2,1,0:T(8,128)S(1)}, f32[16,64,128]{2,1,0:T(8,128)}, u32[]{:S(2)}) %copy-start) | copy-done | bytes 524312
  2.4 0.0 copy-start.1
  2.4 1.0 %copy-done.1 = f32[16,64,128]{2,1,0:T(8,128)S(1)} copy-done((f32[16,64,128]{2,1,0:T(8,128)S(1)}, f32[16,64,128]{2,1,0:T(8,128)}, u32[]{:S(2)}) %copy-start.1) | copy-done | bytes 524312
  3.4 23.2 %shard_map.68 = (f32[48,96,128]{2,1,0:T(8,128)S(1)}, f32[3,2,96,128]{3,2,1,0:T(8,128)S(1)}, f32[3,2,96,128]{3,2,1,0:T(8,128)S(1)}, f32[64,128]{1,0:T(8,128)S(1)}...) custom-call(f32[16,64,128]{2,1,0:T(8,128)S(1)} %copy-done, ...), custom_call_target="tpu_custom_call" | custom-call | tf_op jit(solution)/shard_map/pallas_call | solution.py:609
  26.7 0.8 %jit_solution_.3.wy_ref = f32[5,16,128]{2,1,0:T(8,128)S(1)} broadcast(f32[5,16]{1,0:T(8,128)} %constant.4.clone), dimensions={0,1} | broadcast | bytes 41280 | tf_op jit(solution)
  27.5 0.0 copy-start.2
  27.5 1.0 %copy-done.2 = f32[5,128,128]{2,1,0:T(8,128)S(1)} copy-done((f32[5,128,128]{2,1,0:T(8,128)S(1)}, f32[5,128,128]{2,1,0:T(8,128)}, u32[]{:S(2)}) %copy-start.2) | copy-done | bytes 327704
  28.4 12.8 %shard_map.69.block_ref = f32[56,128]{1,0:T(8,128)S(1)} custom-call(s32[3,2,5,9]{3,2,1,0:T(8,128)S(1)} %copy.7.nodes_ref, f32[48,96,128]{2,1,0:T(8,128)S(1)} %get-tuple-element.11.wide_ref, f32[3,2,96,128]{3,2,1,0:T(8,128)S(1)} %get-tuple-element.12.from_low_ref, f32[3,2,96,128]{3,2,1,0:T(8,128)S(1)} %get-tuple-element.13.from_high_ref, ...), custom_call_target="tpu_custom_call" | custom-call | tf_op jit(solution)/shard_map/pallas_call | solution.py:627
  41.2 20.4 %shard_map.70.gathered_ref = f32[4,2,4,56,128]{4,3,2,1,0:T(8,128)S(1)} custom-call(f32[56,128]{1,0:T(8,128)S(1)} %shard_map.69.block_ref), custom_call_target="tpu_custom_call" | custom-call | tf_op jit(solution)/shard_map/pallas_call | solution.py:647
  61.7 6.9 %shard_map.71 = (f32[3,2,5,9]{3,2,1,0:T(8,128)S(1)}, f32[3,2,5,9]{3,2,1,0:T(8,128)S(1)}) custom-call(f32[4,2,4,56,128]{4,3,2,1,0:T(8,128)S(1)} %shard_map.70.gathered_ref), custom_call_target="tpu_custom_call" | custom-call | tf_op jit(solution)/shard_map/pallas_call | solution.py:660
  68.6 0.6 copy.8
  69.2 0.6 copy.9
Async XLA Ops:
  1.4 1.0 %copy-start = (f32[16,64,128]{2,1,0:T(8,128)S(1)}, f32[16,64,128]{2,1,0:T(8,128)}, u32[]{:S(2)}) copy-start(f32[16,64,128]{2,1,0:T(8,128)} %image_ref.3) | copy-start | bytes 1572868
  2.4 1.0 %copy-start.1 = (f32[16,64,128]{2,1,0:T(8,128)S(1)}, f32[16,64,128]{2,1,0:T(8,128)}, u32[]{:S(2)}) copy-start(f32[16,64,128]{2,1,0:T(8,128)} %deformed_ref.1) | copy-start | bytes 1572868
  27.5 1.0 %copy-start.2 = (f32[5,128,128]{2,1,0:T(8,128)S(1)}, f32[5,128,128]{2,1,0:T(8,128)}, u32[]{:S(2)}) copy-start(f32[5,128,128]{2,1,0:T(8,128)} %constant.5.clone.wx_ref) | copy-start | bytes 983044

commit v3 on v1

v3 whole, which is shorter than its diff:
```python
import functools

import jax
import jax.numpy as jnp
import numpy as np
from jax import lax
from jax.experimental import pallas as pl
from jax.experimental.pallas import tpu as pltpu
from jax.sharding import PartitionSpec as P

ELEM = 16
CGSTEPS = 8
QUANTUM = 64
DAMPING = 0.5
LANES = 128
SLOTS = LANES // ELEM
PAIRS = ((0, 0), (0, 1), (0, 2), (1, 1), (1, 2), (2, 2))
PAIR_OF = ((0, 1, 2), (1, 3, 4), (2, 4, 5))
GROUP = 12
GROUPS = 5
HALF = 8
CHUNKS = 3 * ELEM // HALF

POSITION = (np.arange(ELEM) + 0.5) / ELEM
LINEAR = np.stack([1.0 - POSITION, POSITION])
SQUARED = np.stack([LINEAR[0] * LINEAR[0], LINEAR[0] * LINEAR[1], LINEAR[1] * LINEAR[1]])


def lane_of(shape):
    return lax.broadcasted_iota(jnp.int32, shape, len(shape) - 1)


def pack_face(load, first):
    total = load(0)
    slot = lane_of(total.shape) // ELEM
    total = pltpu.roll(total, (-first) % LANES, 1) if first else total
    for group in range(1, HALF):
        piece = pltpu.roll(load(group), (ELEM * group - first) % LANES, 1)
        total = jnp.where(slot == group, piece, total)
    return total


def flip(index, step):
    return index + step - 2 * step * ((index // step) % 2)


class Gather:
    def __init__(self, ref, send_sem, recv_sem):
        self.ref, self.sems = ref, (send_sem, recv_sem)
        self.sizes = ref.shape[:3]
        size_x, size_y, size_z = self.sizes
        self.at = ix, iy, iz = tuple(lax.axis_index(axis) for axis in ("gx", "gy", "gz"))
        self.steps = []
        step = size_x // 2
        while step:
            self.steps.append(step)
            step //= 2
        self.z_peers = [{"gz": (iz + hop) % size_z} for hop in range(1, size_z)]
        self.y_peers = [{"gy": (iy + hop) % size_y} for hop in range(1, size_y)]
        self.x_peers = [{"gx": flip(ix, step)} for step in self.steps]
        self.peers = self.z_peers + self.y_peers + self.x_peers
        self.sent, self.phase, self.held = [], [], [ix]

    def send(self, source, arriving, peer):
        index = len(self.sent)

        def copy(ref):
            return pltpu.make_async_remote_copy(
                src_ref=ref,
                dst_ref=ref,
                send_sem=self.sems[0].at[index],
                recv_sem=self.sems[1].at[index],
                device_id=peer,
                device_id_type=MESH,
            )

        outgoing = copy(source)
        outgoing.start()
        self.sent.append(outgoing)
        self.phase.append(copy(arriving))

    def arrive(self):
        for copy in self.phase:
            copy.wait_recv()
        self.phase = []

    def start_z(self):
        (ix, iy, iz), size = self.at, self.sizes[2]
        for hop in range(1, size):
            other = (iz + size - hop) % size
            self.send(self.ref.at[ix, iy, iz], self.ref.at[ix, iy, other], self.z_peers[hop - 1])

    def start_y(self):
        (ix, iy, iz), size = self.at, self.sizes[1]
        for hop in range(1, size):
            other = (iy + size - hop) % size
            self.send(self.ref.at[ix, iy], self.ref.at[ix, other], self.y_peers[hop - 1])

    def start_x(self, number):
        step = self.steps[number]
        for own in self.held:
            self.send(self.ref.at[own], self.ref.at[flip(own, step)], self.x_peers[number])
        self.held = self.held + [flip(own, step) for own in self.held]

    def finish(self):
        for copy in self.sent:
            copy.wait_send()


MESH = pl.DeviceIdType.MESH


def neighbour_barrier(sides, peers):
    barrier = pltpu.get_barrier_semaphore()
    count = len(peers)
    for peer in peers:
        pl.semaphore_signal(barrier, inc=1, device_id=peer, device_id_type=MESH)
    for axis, delta, exists in sides:

        @pl.when(exists)
        def _(axis=axis, delta=delta):
            pl.semaphore_signal(
                barrier, inc=1, device_id={axis: lax.axis_index(axis) + delta}, device_id_type=MESH
            )

        count = count + exists.astype(jnp.int32)
    pl.semaphore_wait(barrier, count)


def moments_row(ey, ref_ref, x_low_ref, x_high_ref, wy_ref, u_ref, count_y):
    lane_8 = lane_of((8, LANES))
    sums = []
    for half in range(ELEM // 8):
        squares = [[None] * 3 for _ in PAIRS]
        at = ey * ELEM + 8 * half
        for z in range(ELEM):
            slopes = slopes_at(z, at, ref_ref, x_low_ref, x_high_ref, lane_8)
            for index, (c, d) in enumerate(PAIRS):
                product = slopes[c] * slopes[d]
                for level in range(3):
                    term = float(SQUARED[level, z]) * product
                    squares[index][level] = term if z == 0 else squares[index][level] + term
        sums.append(squares)
    for index in range(len(PAIRS)):
        for level in range(3):
            for t in range(3):
                total = sum(
                    sums[half][index][level] * wy_ref[t, 8 * half : 8 * half + 8, :]
                    for half in range(2)
                )
                kind = index * 9 + level * 3 + t
                u_ref[pl.ds(kind * count_y + ey, 1), :] = jnp.sum(total, axis=0, keepdims=True)


def slopes_at(z, at, ref_ref, x_low_ref, x_high_ref, lane_8):
    group, part = z % HALF, z // HALF
    at = pl.multiple_of(at, 8)
    row = pl.multiple_of(at + 8, 8)
    here = ref_ref[z + 1, pl.ds(row, 8), :]
    left = jnp.where(
        lane_8 == 0,
        pltpu.roll(x_low_ref[part, pl.ds(at, 8), :], (2 * LANES - ELEM * group - ELEM + 1) % LANES, 1),
        pltpu.roll(here, 1, 1),
    )
    right = jnp.where(
        lane_8 == LANES - 1,
        pltpu.roll(x_high_ref[part, pl.ds(at, 8), :], (LANES - 1 - ELEM * group) % LANES, 1),
        pltpu.roll(here, LANES - 1, 1),
    )
    return (
        0.5 * (ref_ref[z + 2, pl.ds(row, 8), :] - ref_ref[z, pl.ds(row, 8), :]),
        0.5 * (ref_ref[z + 1, pl.ds(at + 9, 8), :] - ref_ref[z + 1, pl.ds(at + 7, 8), :]),
        0.5 * (right - left),
    )


def contract_x(u_ref, wx_ref, rows):
    total = 0.0
    for group in range(wx_ref.shape[0]):
        total = total + jnp.dot(
            u_ref[group * rows : (group + 1) * rows, :],
            wx_ref[group],
            precision=lax.Precision.HIGHEST,
            preferred_element_type=jnp.float32,
        )
    return total


def halo_kernel(
    image_ref, deformed_ref, wy_ref, wx_ref,
    wide_ref, from_low_ref, from_high_ref, ref_ref, x_low_ref, x_high_ref, gathered_ref,
    to_low_ref, to_high_ref, ref_low_ref, ref_high_ref, u_ref,
    z_low_ref, z_high_ref, y_low_ref, y_high_ref, send_sem, recv_sem, gather_send, gather_recv,
):
    size_z, size_y, _ = image_ref.shape
    count_y = size_y // ELEM
    low, high = {}, {}
    for axis in ("gz", "gy", "gx"):
        low[axis] = lax.axis_index(axis) > 0
        high[axis] = lax.axis_index(axis) < lax.axis_size(axis) - 1
    sides = [(axis, -1, low[axis]) for axis in low] + [(axis, 1, high[axis]) for axis in high]
    gather = Gather(gathered_ref, gather_send, gather_recv)
    neighbour_barrier(sides, gather.peers)
    copies = []

    def send(axis, delta, source, target):
        index = len(copies)
        copy = pltpu.make_async_remote_copy(
            src_ref=source,
            dst_ref=target,
            send_sem=send_sem.at[index],
            recv_sem=recv_sem.at[index],
            device_id={axis: lax.axis_index(axis) + delta},
            device_id_type=MESH,
        )
        sends, receives = (high[axis], low[axis]) if delta > 0 else (low[axis], high[axis])
        copies.append((copy, sends))

        @pl.when(sends)
        def _():
            copy.start()

        def arrive():
            @pl.when(receives)
            def _():
                copy.wait_recv()

        def blank(*refs):
            @pl.when(jnp.logical_not(receives))
            def _():
                for ref in refs:
                    ref[...] = jnp.zeros(ref.shape, ref.dtype)

        arrive.blank = blank
        return arrive

    rows = pl.ds(ELEM, size_y)
    middle = pl.ds(ELEM, ELEM)
    first_rows, last_rows = pl.ds(0, ELEM), pl.ds(size_y - ELEM, ELEM)
    into_low, into_high = pl.ds(0, ELEM), pl.ds(ELEM + size_y, ELEM)
    others = [
        send("gz", 1, image_ref.at[size_z - 1], z_low_ref),
        send("gz", -1, image_ref.at[0], z_high_ref),
        send("gy", 1, image_ref.at[:, pl.ds(size_y - 8, 8)], y_low_ref),
        send("gy", -1, image_ref.at[:, pl.ds(0, 8)], y_high_ref),
    ]
    waits = []
    for half in range(ELEM // HALF):
        depth = pl.ds(half * HALF, HALF)
        waits.append(
            [
                send("gz", 1, deformed_ref.at[depth], wide_ref.at[depth, rows]),
                send("gz", -1, deformed_ref.at[depth], wide_ref.at[pl.ds(2 * ELEM + half * HALF, HALF), rows]),
            ]
        )
    center = [
        send("gy", 1, deformed_ref.at[:, last_rows], wide_ref.at[middle, into_low]),
        send("gy", -1, deformed_ref.at[:, first_rows], wide_ref.at[middle, into_high]),
    ]
    for first, face in ((0, ref_low_ref), (LANES - ELEM, ref_high_ref)):
        for half in range(ELEM // HALF):
            face[half] = pack_face(lambda z: image_ref[half * HALF + z], first)
    others += [
        send("gx", 1, ref_high_ref, x_low_ref),
        send("gx", -1, ref_low_ref, x_high_ref),
    ]
    for arrive, ref in zip(
        others, (z_low_ref, z_high_ref, y_low_ref, y_high_ref, x_low_ref, x_high_ref)
    ):
        arrive.blank(ref)
    waits[0][0].blank(wide_ref.at[pl.ds(0, ELEM), rows])
    waits[0][1].blank(wide_ref.at[pl.ds(2 * ELEM, ELEM), rows])
    wide_ref[middle, rows] = deformed_ref[...]
    ref_ref[1 : 1 + size_z, 8 : 8 + size_y] = image_ref[...]
    u_ref[...] = jnp.zeros_like(u_ref)

    final = []

    def x_faces(chunks, arrivals):
        start = pl.ds(chunks[0] * HALF, len(chunks) * HALF)
        arrivals[0].blank(wide_ref.at[start, into_low])
        arrivals[1].blank(wide_ref.at[start, into_high])
        for arrive in arrivals:
            arrive()
        for chunk in chunks:
            for first, face in ((0, to_low_ref), (LANES - ELEM, to_high_ref)):
                face[chunk] = pack_face(lambda z: wide_ref[chunk * HALF + z], first)
            pair = [
                send("gx", 1, to_high_ref.at[chunk], from_low_ref.at[chunk]),
                send("gx", -1, to_low_ref.at[chunk], from_high_ref.at[chunk]),
            ]
            pair[0].blank(from_low_ref.at[chunk])
            pair[1].blank(from_high_ref.at[chunk])
            final.extend(pair)

    def forward_y(half):
        result = []
        for side in range(2):
            waits[half][side]()
            chunk = side * 2 * (ELEM // HALF) + half
            depth = pl.ds(chunk * HALF, HALF)
            result.append(
                (
                    chunk,
                    [
                        send("gy", 1, wide_ref.at[depth, pl.ds(size_y, ELEM)], wide_ref.at[depth, into_low]),
                        send("gy", -1, wide_ref.at[depth, pl.ds(ELEM, ELEM)], wide_ref.at[depth, into_high]),
                    ],
                )
            )
        return result

    for arrive in others:
        arrive()
    ref_ref[0, 8 : 8 + size_y] = z_low_ref[...]
    ref_ref[size_z + 1, 8 : 8 + size_y] = z_high_ref[...]
    ref_ref[1 : 1 + size_z, 0:8] = y_low_ref[...]
    ref_ref[1 : 1 + size_z, 8 + size_y : 16 + size_y] = y_high_ref[...]

    def moments(ey, carry):
        moments_row(ey, ref_ref, x_low_ref, x_high_ref, wy_ref, u_ref, count_y)
        return carry

    lax.fori_loop(0, count_y // 2, moments, 0)
    x_faces((2, 3), center)
    early = forward_y(0)
    lax.fori_loop(count_y // 2, count_y, moments, 0)
    gathered_ref[gather.at[0], gather.at[1], gather.at[2]] = contract_x(
        u_ref, wx_ref, GROUP * count_y
    )
    gather.start_z()
    for chunk, arrivals in early:
        x_faces((chunk,), arrivals)
    late = forward_y(1)
    gather.arrive()
    gather.start_y()
    for chunk, arrivals in late:
        x_faces((chunk,), arrivals)
    gather.arrive()
    for number in range(len(gather.steps)):
        gather.start_x(number)
        gather.arrive()
    for arrive in final:
        arrive()
    gather.finish()
    for copy, sends in copies:

        @pl.when(sends)
        def _(copy=copy):
            copy.wait_send()


HALO_COPIES = 4 + 2 * (ELEM // HALF) + 2 + 2 + 4 * (ELEM // HALF) + 2 * CHUNKS


def gather_kernel(block_ref, gathered_ref, send_sem, recv_sem):
    gather = Gather(gathered_ref, send_sem, recv_sem)
    neighbour_barrier([], gather.peers)
    gathered_ref[gather.at[0], gather.at[1], gather.at[2]] = block_ref[...]
    gather.start_z()
    gather.arrive()
    gather.start_y()
    gather.arrive()
    for number in range(len(gather.steps)):
        gather.start_x(number)
        gather.arrive()
    gather.finish()


def element_kernel(
    nodes_ref, wide_ref, from_low_ref, from_high_ref, ref_ref, x_low_ref, x_high_ref,
    wy_ref, wx_ref, out_ref, low_ref, high_ref, warp_ref, u_ref,
):
    rows_wide = wide_ref.shape[1]
    size_y = rows_wide - 2 * ELEM
    count_y, count_x = size_y // ELEM, LANES // ELEM
    lane_wide = lane_of((rows_wide, LANES))

    def spread(chunk, carry):
        left, right = from_low_ref[chunk], from_high_ref[chunk]
        for group in range(HALF):
            z = chunk * HALF + group
            centre = wide_ref[z]
            low = pltpu.roll(left, (2 * LANES - ELEM - ELEM * group) % LANES, 1)
            low_ref[z] = jnp.where(lane_wide >= LANES - ELEM, low, centre)
            high = pltpu.roll(right, (LANES - ELEM * group) % LANES, 1)
            high_ref[z] = jnp.where(lane_wide < ELEM, high, centre)
        return carry

    lax.fori_loop(0, CHUNKS, spread, 0)

    lane_16 = lane_of((ELEM, LANES))
    lane_8 = lane_of((8, LANES))

    def row(ey, carry):
        base = pl.multiple_of(ey * ELEM, ELEM)

        def element(source, ex):
            starts, shares = [], []
            for c in range(3):
                total = 0
                for offset in range(8):
                    total = total + nodes_ref[
                        c, offset >> 2, ey + (offset >> 1 & 1), ex + (offset & 1)
                    ]
                starts.append((total >> 9) + ELEM)
                shares.append((total & 511).astype(jnp.float32) * (1.0 / (8 * QUANTUM)))
            sz, sy, sx = starts
            fz, fy, fx = shares
            ys = base + sy
            back = (2 * LANES + ELEM - sx) % LANES
            back_next = (2 * LANES + ELEM - 1 - sx) % LANES
            mine = lane_16 // ELEM == ex

            def plane(z):
                return (1.0 - fy) * source[sz + z, pl.ds(ys, ELEM), :] + fy * source[
                    sz + z, pl.ds(ys + 1, ELEM), :
                ]

            before = plane(0)
            for z in range(ELEM):
                after = plane(z + 1)
                mixed = (1.0 - fz) * before + fz * after
                before = after
                value = (1.0 - fx) * pltpu.roll(mixed, back, 1) + fx * pltpu.roll(
                    mixed, back_next, 1
                )
                warp_ref[z] = jnp.where(mine, value, warp_ref[z])

        element(low_ref, 0)

        def middle(ex, carry):
            element(wide_ref, ex)
            return carry

        lax.fori_loop(1, count_x - 1, middle, 0)
        element(high_ref, count_x - 1)

        sums = []
        for half in range(ELEM // 8):
            loads = [[None] * 2 for _ in range(3)]
            at = base + 8 * half
            for z in range(ELEM):
                slopes = slopes_at(z, at, ref_ref, x_low_ref, x_high_ref, lane_8)
                here = ref_ref[z + 1, pl.ds(pl.multiple_of(at + 8, 8), 8), :]
                mismatch = here - warp_ref[z, 8 * half : 8 * half + 8, :]
                for c in range(3):
                    product = slopes[c] * mismatch
                    for a in range(2):
                        term = float(LINEAR[a, z]) * product
                        loads[c][a] = term if z == 0 else loads[c][a] + term
            sums.append(loads)
        for c in range(3):
            for a in range(2):
                for b in range(2):
                    total = sum(
                        sums[half][c][a] * wy_ref[3 + b, 8 * half : 8 * half + 8, :]
                        for half in range(2)
                    )
                    kind = c * 4 + a * 2 + b
                    u_ref[pl.ds(kind * count_y + ey, 1), :] = jnp.sum(total, axis=0, keepdims=True)
        return carry

    lax.fori_loop(0, count_y, row, 0)
    out_ref[...] = contract_x(u_ref, wx_ref, out_ref.shape[0])


def cg_kernel(axes, gathered_ref, loads_ref, update_ref, residual_ref, m_ref, b_ref, s_ref, r_ref, d_ref):
    count_x, count_y = axes
    groups_x, groups_y, groups_z = gathered_ref.shape[:3]
    places = groups_z * groups_x
    total_y = groups_y * count_y
    elems_x = lax.axis_size("gx") * count_x
    shape = (total_y, LANES)
    lane = lane_of(shape)
    line = lax.broadcasted_iota(jnp.int32, shape, 0)
    slot = lane // count_x
    per = 8 // count_y

    def unpack(source, target, lines, pair, carry):
        at = pl.multiple_of(pair * 8, 8)
        tiles = [
            [
                source[j % groups_x, iy, j // groups_x, pl.ds(at, 8), :]
                for iy in range(groups_y)
            ]
            for j in range(places)
        ]
        for half in range(per):
            values = [
                jnp.concatenate(
                    [tile[half * count_y : (half + 1) * count_y] for tile in tiles[j]], axis=0
                )
                for j in range(places)
            ]
            step = 1
            while step < places:
                bit = (slot // step) % 2 == 0
                fresh = list(values)
                for j in range(places):
                    if (j // step) % 2 == 0:
                        first, second = values[j], values[j + step]
                        fresh[j] = jnp.where(bit, first, pltpu.roll(second, step * count_x, 1))
                        fresh[j + step] = jnp.where(
                            bit, pltpu.roll(first, LANES - step * count_x, 1), second
                        )
                values = fresh
                step *= 2
            for high in range(places):
                target[high * lines + pair * per + half] = values[high]
        return carry

    lax.fori_loop(0, GROUP // per, functools.partial(unpack, gathered_ref, m_ref, GROUP), 0)
    unpack(loads_ref, b_ref, per, 0, 0)

    edge = {
        2: (lane % elems_x == 0, lane % elems_x == elems_x - 1, 1, 1),
        1: (line == 0, line == total_y - 1, 1, 0),
        0: (lane < elems_x, lane >= LANES - elems_x, elems_x, 1),
    }
    corner_list = [(a, b, g) for a in range(2) for b in range(2) for g in range(2)]
    keys = [(c,) + k for c in range(3) for k in corner_list]
    position = {key: index for index, key in enumerate(keys)}
    one = jnp.ones(shape, jnp.float32)
    own = {}
    for corner in corner_list:
        mask = one
        for dim in range(3):
            if corner[dim]:
                mask = jnp.where(edge[dim][1], mask, 0.0)
        own[corner] = mask

    def assemble(parts):
        for dim in range(3):
            first, last, shift, axis = edge[dim]
            extent = shape[axis]
            fresh = {}
            for key in keys:
                if key[1 + dim] == 0:
                    other = key[: 1 + dim] + (1,) + key[2 + dim :]
                    low, high = parts[key], parts[other]
                    fresh[key] = low + jnp.where(first, 0.0, pltpu.roll(high, shift, axis))
                    fresh[other] = high + jnp.where(last, 0.0, pltpu.roll(low, extent - shift, axis))
            parts = fresh
        return parts

    def squares(parts):
        total = {}
        for corner in corner_list:
            total[corner] = sum(parts[(c,) + corner] * parts[(c,) + corner] for c in range(3))
        return sum(total[corner] * own[corner] for corner in corner_list)

    parts = {}
    for c, a, b, g in keys:
        kind = c * 4 + a * 2 + b
        parts[c, a, b, g] = b_ref[((kind // per) * 2 + g) * per + kind % per]
    parts = assemble(parts)
    for key in keys:
        s_ref[position[key]] = jnp.zeros(shape, jnp.float32)
        r_ref[position[key]] = parts[key]
        d_ref[position[key]] = parts[key]

    def step(index, norm_now):
        d = {key: d_ref[position[key]] for key in keys}
        image = {key: None for key in keys}
        for p, (first, second) in enumerate(PAIRS):
            orders = ((first, second),) if first == second else ((first, second), (second, first))
            for s in range(3):
                for t in range(3):
                    for u in range(3):
                        kind = p * 9 + s * 3 + t
                        value = m_ref[((kind // GROUP) * 3 + u) * GROUP + kind % GROUP]
                        for c, e in orders:
                            for a, b, g in corner_list:
                                q = (s - a, t - b, u - g)
                                if min(q) < 0 or max(q) > 1:
                                    continue
                                term = value * d[(e,) + q]
                                key = (c, a, b, g)
                                image[key] = term if image[key] is None else image[key] + term
        dots = sum(image[key] * d[key] for key in keys) + DAMPING * squares(d)
        alpha = norm_now / jnp.sum(dots)
        image = assemble(image)
        residual = {}
        for key in keys:
            at = position[key]
            s_ref[at] = s_ref[at] + alpha * d[key]
            residual[key] = r_ref[at] - alpha * (image[key] + DAMPING * d[key])
            r_ref[at] = residual[key]
        norm_next = jnp.sum(squares(residual))
        beta = norm_next / norm_now
        for key in keys:
            d_ref[position[key]] = residual[key] + beta * d[key]
        return norm_next

    start = {key: r_ref[position[key]] for key in keys}
    lax.fori_loop(0, CGSTEPS, step, jnp.sum(squares(start)))

    place = lax.axis_index("gz") * lax.axis_size("gx") + lax.axis_index("gx")
    first_lane = place * count_x
    first_line = lax.axis_index("gy") * count_y
    last_lane = (first_lane + count_x) % LANES
    last_line = (first_line + count_y) % total_y
    for source, out, scale in ((s_ref, update_ref, float(QUANTUM)), (r_ref, residual_ref, 1.0)):
        for c in range(3):
            for a in range(2):
                merged = []
                for b in range(2):
                    merged.append(
                        jnp.where(
                            lane == last_lane,
                            pltpu.roll(source[position[c, a, b, 1]], 1, 1),
                            source[position[c, a, b, 0]],
                        )
                    )
                value = jnp.where(line == last_line, pltpu.roll(merged[1], 1, 0), merged[0])
                value = pltpu.roll(value, (LANES - first_lane) % LANES, 1)
                value = pltpu.roll(value, (total_y - first_line) % total_y, 0)
                out[c, a] = scale * value[: count_y + 1, : count_x + 1]


def x_weights(count_x, weights, groups):
    table = np.zeros((groups, LANES, LANES), np.float32)
    for group in range(groups):
        for u, weight in enumerate(weights):
            for k in range(count_x):
                column = (group * len(weights) + u) * count_x + k
                table[group, k * ELEM : (k + 1) * ELEM, column] = weight / ELEM**2
    return jnp.asarray(table)


def y_weights():
    table = np.concatenate([SQUARED, LINEAR]).astype(np.float32)
    return jnp.asarray(np.broadcast_to(table[:, :, None], table.shape + (LANES,)))


VMEM = pl.BlockSpec(memory_space=pltpu.VMEM)
SMEM = pl.BlockSpec(memory_space=pltpu.SMEM)
PARAMS = pltpu.CompilerParams(vmem_limit_bytes=48 * 2**20)


def per_device(ref_image, deformed_image, nodal_disp):
    size_z, size_y, size_x = ref_image.shape
    count_y, count_x = size_y // ELEM, size_x // ELEM
    f32 = jnp.float32
    per = 8 // count_y
    load_groups = 12 // per
    sizes = tuple(lax.axis_size(axis) for axis in ("gx", "gy", "gz"))
    groups = sizes[0] * sizes[2]
    gather_sems = pltpu.SemaphoreType.DMA((sum(sizes) - 3,))
    moments = jax.ShapeDtypeStruct(sizes + (GROUP * count_y, LANES), f32)
    wide = jax.ShapeDtypeStruct((3 * ELEM, size_y + 2 * ELEM, LANES), f32)
    face = jax.ShapeDtypeStruct((CHUNKS, size_y + 2 * ELEM, LANES), f32)
    ref_face = jax.ShapeDtypeStruct((ELEM // HALF, size_y, LANES), f32)
    padded = jax.ShapeDtypeStruct((size_z + 2, size_y + 16, LANES), f32)
    plane = pltpu.VMEM((size_y, LANES), f32)
    edge = pltpu.VMEM((size_z, 8, LANES), f32)
    by_y = y_weights()
    *halos, gathered = pl.pallas_call(
        halo_kernel,
        out_shape=(wide, face, face, padded, ref_face, ref_face, moments),
        in_specs=[VMEM] * 4,
        out_specs=[VMEM] * 7,
        scratch_shapes=[
            pltpu.VMEM(face.shape, f32),
            pltpu.VMEM(face.shape, f32),
            pltpu.VMEM(ref_face.shape, f32),
            pltpu.VMEM(ref_face.shape, f32),
            pltpu.VMEM((GROUP * GROUPS * count_y, LANES), f32),
            plane,
            plane,
            edge,
            edge,
            pltpu.SemaphoreType.DMA((HALO_COPIES,)),
            pltpu.SemaphoreType.DMA((HALO_COPIES,)),
            gather_sems,
            gather_sems,
        ],
        compiler_params=pltpu.CompilerParams(
            vmem_limit_bytes=48 * 2**20, collective_id=0, has_side_effects=True
        ),
    )(ref_image, deformed_image, by_y, x_weights(count_x, SQUARED, GROUPS))
    block = pl.pallas_call(
        element_kernel,
        out_shape=jax.ShapeDtypeStruct((8, LANES), f32),
        in_specs=[SMEM] + [VMEM] * 8,
        out_specs=VMEM,
        scratch_shapes=[
            pltpu.VMEM(wide.shape, f32),
            pltpu.VMEM(wide.shape, f32),
            pltpu.VMEM((ELEM, ELEM, LANES), f32),
            pltpu.VMEM((12 * count_y, LANES), f32),
        ],
        compiler_params=PARAMS,
    )(nodal_disp, *halos, by_y, x_weights(count_x, LINEAR, load_groups))
    loads = pl.pallas_call(
        gather_kernel,
        out_shape=jax.ShapeDtypeStruct(sizes + block.shape, f32),
        in_specs=[VMEM],
        out_specs=VMEM,
        scratch_shapes=[gather_sems, gather_sems],
        compiler_params=pltpu.CompilerParams(
            vmem_limit_bytes=48 * 2**20, collective_id=1, has_side_effects=True
        ),
    )(block)
    total_y = lax.axis_size("gy") * count_y
    fields = pltpu.VMEM((24, total_y, LANES), f32)
    nodes_out = jax.ShapeDtypeStruct(nodal_disp.shape, f32)
    return pl.pallas_call(
        functools.partial(cg_kernel, (count_x, count_y)),
        out_shape=(nodes_out, nodes_out),
        in_specs=[VMEM] * 2,
        out_specs=[VMEM] * 2,
        scratch_shapes=[
            pltpu.VMEM((groups * GROUP, total_y, LANES), f32),
            pltpu.VMEM((groups * per, total_y, LANES), f32),
            fields,
            fields,
            fields,
        ],
        compiler_params=PARAMS,
    )(gathered, loads)


def solution(mesh):
    in_specs = (P("gz", "gy", "gx"), P("gz", "gy", "gx"), P(None, "gz", "gy", "gx"))
    out_specs = (P(None, "gz", "gy", "gx"), P(None, "gz", "gy", "gx"))
    return jax.shard_map(
        per_device, mesh=mesh, in_specs=in_specs, out_specs=out_specs, check_vma=False
    )
```

time: 150 us -> 67 us (0.45)
  blocking collectives: 70 us -> 0 us
  Pallas kernels: 21.1 us -> 59.2 us
  starting transfers between devices: 29.1 us -> 0 us
  waiting for transfers between devices: 25.8 us -> 0 us
  local copies, waits for them, and re-layouts: 2.55 us -> 6.76 us
    all_gather x1 -> x0, blocking collectives: 70 us -> none  [per_device(): gathered = lax.all_gather(block, ('gz', 'gx', 'gy'), axis=0)]
    pallas_call x3 -> x4, Pallas kernels: 21.1 us -> 59.2 us  [the longest x1 31.2 us: per_device(): pl.pallas_call(halo_kernel, out_shape=(wide, face, face, padded, ref_face...]
    ppermute x12 -> x0, starting transfers between devices: 29.1 us -> none  [the longest x6 21.3 us: exchange(): lax.ppermute(to_high, axis, forward)]
    ppermute x12 -> x0, waiting for transfers between devices: 25.8 us -> none  [the longest x6 13.5 us: exchange(): lax.ppermute(to_low, axis, backward)]
    unnamed x11 -> x9, local copies, waits for them, and re-layouts: 1.15 us -> 4.78 us
  transfers between devices with their start and end apart: 12 -> 0, of which waited for: 7 -> 0; matrix products, arithmetic and copies ran while one was open for 1% -> 0% of each run, Pallas kernels for 1% -> 0%
where the time goes in v3:
time: 67 us; the launch traced here: 66.7 us
  Pallas kernels  59.2 us (88%)
  local copies, waits for them, and re-layouts  6.76 us (10%)
    pallas_call x1, Pallas kernels, per_device(): pl.pallas_call(halo_kernel, out_shape=(wide, face, face, padded, ref_face...  31.2 us
    pallas_call x1, Pallas kernels, per_device(): pl.pallas_call(gather_kernel, out_shape=jax.ShapeDtypeStruct(sizes + bloc...  12.2 us
    pallas_call x1, Pallas kernels, per_device(): pl.pallas_call(element_kernel, out_shape=jax.ShapeDtypeStruct((8, LANES),...  8.87 us
    pallas_call x1, Pallas kernels, per_device(): pl.pallas_call(functools.partial(cg_kernel, (count_x, count_y)), out_shap...  6.9 us
    unnamed x9, local copies, waits for them, and re-layouts  4.78 us

profile of v3, /device:TPU:0, one launch (start us, length us, event | category | flops | bytes accessed | tf_op | source)
XLA Modules:
  0.0 66.7 jit_solution(2015792494878357382)
XLA Ops:
  0.6 0.8 %jit_solution_.3.wy_ref = f32[5,16,128]{2,1,0:T(8,128)S(1)} broadcast(f32[5,16]{1,0:T(8,128)} %constant.6.clone), dimensions={0,1} | broadcast | bytes 41280 | tf_op jit(solution)
  1.4 0.0 copy-start
  1.4 1.0 %copy-done = f32[16,64,128]{2,1,0:T(8,128)S(1)} copy-done((f32[16,64,128]{2,1,0:T(8,128)S(1)}, f32[16,64,128]{2,1,0:T(8,128)}, u32[]{:S(2)}) %copy-start) | copy-done | bytes 524312
  2.4 0.0 copy-start.1
  2.4 1.0 %copy-done.1 = f32[16,64,128]{2,1,0:T(8,128)S(1)} copy-done((f32[16,64,128]{2,1,0:T(8,128)S(1)}, f32[16,64,128]{2,1,0:T(8,128)}, u32[]{:S(2)}) %copy-start.1) | copy-done | bytes 524312
  3.5 0.0 copy-start.3
  3.5 1.0 %copy-done.3 = f32[5,128,128]{2,1,0:T(8,128)S(1)} copy-done((f32[5,128,128]{2,1,0:T(8,128)S(1)}, f32[5,128,128]{2,1,0:T(8,128)}, u32[]{:S(2)}) %copy-start.3) | copy-done | bytes 327704
  4.5 31.2 %shard_map.77 = (f32[48,96,128]{2,1,0:T(8,128)S(1)}, f32[6,96,128]{2,1,0:T(8,128)S(1)}, f32[6,96,128]{2,1,0:T(8,128)S(1)}, f32[18,80,128]{2,1,0:T(8,128)S(1)}, f...) custom-call(f32[16,64,128]{2,1,0:T(8,128)S(1)} %copy-done, ...), custom_call_target="tpu_custom_call" | custom-call | tf_op jit(solution)/shard_map/pallas_call | solution.py:659
  35.7 0.7 %copy.8.nodes_ref = s32[3,2,5,9]{3,2,1,0:T(8,128)S(1)} copy(s32[3,2,5,9]{3,1,2,0:T(2,128)} %param.8) | data formatting | bytes 2160 | tf_op args[2]
  36.4 0.0 copy-start.2
  36.4 1.0 %copy-done.2 = f32[6,128,128]{2,1,0:T(8,128)S(1)} copy-done((f32[6,128,128]{2,1,0:T(8,128)S(1)}, f32[6,128,128]{2,1,0:T(8,128)}, u32[]{:S(2)}) %copy-start.2) | copy-done | bytes 393240
  37.4 8.9 %shard_map.78.block_ref = f32[8,128]{1,0:T(8,128)S(1)} custom-call(s32[3,2,5,9]{3,2,1,0:T(8,128)S(1)} %copy.8.nodes_ref, f32[48,96,128]{2,1,0:T(8,128)S(1)} %get-tuple-element.10.wide_ref, f32[6,96,128]{2,1,0:T(8,128)S(1)} %get-tuple-element.11.from_low_ref, f32[6,96,128]{2,1,0:T(8,128)S(1)} %get-tuple-element.12.from_high_ref, ...), custom_call_target="tpu_custom_call" | custom-call | tf_op jit(solution)/shard_map/pallas_call | solution.py:683
  46.3 12.2 %shard_map.79.loads_ref = f32[4,2,4,8,128]{4,3,2,1,0:T(8,128)S(1)} custom-call(f32[8,128]{1,0:T(8,128)S(1)} %shard_map.78.block_ref), custom_call_target="tpu_custom_call" | custom-call | tf_op jit(solution)/shard_map/pallas_call | solution.py:696
  58.5 6.9 %shard_map.80 = (f32[3,2,5,9]{3,2,1,0:T(8,128)S(1)}, f32[3,2,5,9]{3,2,1,0:T(8,128)S(1)}) custom-call(f32[4,2,4,48,128]{4,3,2,1,0:T(8,128)S(1)} %get-tuple-element.9.gathered_ref, f32[4,2,4,8,128]{4,3,2,1,0:T(8,128)S(1)} %shard_map.79.loads_ref), custom_call_target="tpu_custom_call" | custom-call | tf_op jit(solution)/shard_map/pallas_call | solution.py:709
  65.4 0.6 copy.9
  66.0 0.6 copy.10
Async XLA Ops:
  1.4 1.0 %copy-start = (f32[16,64,128]{2,1,0:T(8,128)S(1)}, f32[16,64,128]{2,1,0:T(8,128)}, u32[]{:S(2)}) copy-start(f32[16,64,128]{2,1,0:T(8,128)} %image_ref.1) | copy-start | bytes 1572868
  2.4 1.0 %copy-start.1 = (f32[16,64,128]{2,1,0:T(8,128)S(1)}, f32[16,64,128]{2,1,0:T(8,128)}, u32[]{:S(2)}) copy-start(f32[16,64,128]{2,1,0:T(8,128)} %deformed_ref.1) | copy-start | bytes 1572868
  3.5 1.0 %copy-start.3 = (f32[5,128,128]{2,1,0:T(8,128)S(1)}, f32[5,128,128]{2,1,0:T(8,128)}, u32[]{:S(2)}) copy-start(f32[5,128,128]{2,1,0:T(8,128)} %constant.7.clone.wx_ref) | copy-start | bytes 983044
  36.4 1.0 %copy-start.2 = (f32[6,128,128]{2,1,0:T(8,128)S(1)}, f32[6,128,128]{2,1,0:T(8,128)}, u32[]{:S(2)}) copy-start(f32[6,128,128]{2,1,0:T(8,128)} %constant.8.clone.wx_ref) | copy-start | bytes 1179652

commit v4 on v3

--- a/solution.py
+++ b/solution.py
@@ -127,7 +127,33 @@
     pl.semaphore_wait(barrier, count)
 
 
-def moments_row(ey, ref_ref, x_low_ref, x_high_ref, wy_ref, u_ref, count_y):
+def ramp(shape, axis):
+    index = lax.broadcasted_iota(jnp.int32, shape, axis) % ELEM
+    return (index.astype(jnp.float32) + 0.5) * (1.0 / ELEM)
+
+
+def powers(position, squared):
+    rest = 1.0 - position
+    if squared:
+        return (rest * rest, rest * position, position * position)
+    return (rest, position)
+
+
+def x_weights(group, squared):
+    shape = (LANES, LANES)
+    count_x = LANES // ELEM
+    row, column = (lax.broadcasted_iota(jnp.int32, shape, axis) for axis in (0, 1))
+    weights = powers(ramp(shape, 0), squared)
+    total = jnp.zeros(shape, jnp.float32)
+    for u, weight in enumerate(weights):
+        slot = group * len(weights) + u
+        mine = jnp.logical_and(column // count_x == slot, row // ELEM == column % count_x)
+        total = jnp.where(mine, weight * (1.0 / ELEM**2), total)
+    return total
+
+
+def moments_row(ey, ref_ref, x_low_ref, x_high_ref, u_ref, count_y):
+    by_y = powers(ramp((ELEM, LANES), 0), True)
     lane_8 = lane_of((8, LANES))
     sums = []
     for half in range(ELEM // 8):
@@ -145,7 +171,7 @@
         for level in range(3):
             for t in range(3):
                 total = sum(
-                    sums[half][index][level] * wy_ref[t, 8 * half : 8 * half + 8, :]
+                    sums[half][index][level] * by_y[t][8 * half : 8 * half + 8, :]
                     for half in range(2)
                 )
                 kind = index * 9 + level * 3 + t
@@ -174,12 +200,12 @@
     )
 
 
-def contract_x(u_ref, wx_ref, rows):
+def contract_x(u_ref, squared, rows):
     total = 0.0
-    for group in range(wx_ref.shape[0]):
+    for group in range(u_ref.shape[0] // rows):
         total = total + jnp.dot(
             u_ref[group * rows : (group + 1) * rows, :],
-            wx_ref[group],
+            x_weights(group, squared),
             precision=lax.Precision.HIGHEST,
             preferred_element_type=jnp.float32,
         )
@@ -187,7 +213,7 @@
 
 
 def halo_kernel(
-    image_ref, deformed_ref, wy_ref, wx_ref,
+    image_ref, deformed_ref,
     wide_ref, from_low_ref, from_high_ref, ref_ref, x_low_ref, x_high_ref, gathered_ref,
     to_low_ref, to_high_ref, ref_low_ref, ref_high_ref, u_ref,
     z_low_ref, z_high_ref, y_low_ref, y_high_ref, send_sem, recv_sem, gather_send, gather_recv,
@@ -318,7 +344,7 @@
     ref_ref[1 : 1 + size_z, 8 + size_y : 16 + size_y] = y_high_ref[...]
 
     def moments(ey, carry):
-        moments_row(ey, ref_ref, x_low_ref, x_high_ref, wy_ref, u_ref, count_y)
+        moments_row(ey, ref_ref, x_low_ref, x_high_ref, u_ref, count_y)
         return carry
 
     lax.fori_loop(0, count_y // 2, moments, 0)
@@ -326,7 +352,7 @@
     early = forward_y(0)
     lax.fori_loop(count_y // 2, count_y, moments, 0)
     gathered_ref[gather.at[0], gather.at[1], gather.at[2]] = contract_x(
-        u_ref, wx_ref, GROUP * count_y
+        u_ref, True, GROUP * count_y
     )
     gather.start_z()
     for chunk, arrivals in early:
@@ -354,22 +380,51 @@
 
 
 def gather_kernel(block_ref, gathered_ref, send_sem, recv_sem):
-    gather = Gather(gathered_ref, send_sem, recv_sem)
-    neighbour_barrier([], gather.peers)
-    gathered_ref[gather.at[0], gather.at[1], gather.at[2]] = block_ref[...]
-    gather.start_z()
-    gather.arrive()
-    gather.start_y()
-    gather.arrive()
-    for number in range(len(gather.steps)):
-        gather.start_x(number)
-        gather.arrive()
-    gather.finish()
+    sizes = gathered_ref.shape[:3]
+    at = tuple(lax.axis_index(axis) for axis in ("gx", "gy", "gz"))
+    hops = [
+        (x, y, z)
+        for z in range(sizes[2])
+        for y in range(sizes[1])
+        for x in range(sizes[0])
+        if x or y or z
+    ]
+
+    def away(hop, sign):
+        return tuple((at[i] + sizes[i] + sign * hop[i]) % sizes[i] for i in range(3))
+
+    targets = [away(hop, 1) for hop in hops]
+    peers = [dict(zip(("gx", "gy", "gz"), target)) for target in targets]
+    neighbour_barrier([], peers)
+    outgoing = []
+    for index, peer in enumerate(peers):
+        copy = pltpu.make_async_remote_copy(
+            src_ref=block_ref,
+            dst_ref=gathered_ref.at[at],
+            send_sem=send_sem.at[index],
+            recv_sem=recv_sem.at[index],
+            device_id=peer,
+            device_id_type=MESH,
+        )
+        copy.start()
+        outgoing.append(copy)
+    gathered_ref[at] = block_ref[...]
+    for index, hop in enumerate(hops):
+        pltpu.make_async_remote_copy(
+            src_ref=block_ref,
+            dst_ref=gathered_ref.at[away(hop, -1)],
+            send_sem=send_sem.at[index],
+            recv_sem=recv_sem.at[index],
+            device_id=peers[index],
+            device_id_type=MESH,
+        ).wait_recv()
+    for copy in outgoing:
+        copy.wait_send()
 
 
 def element_kernel(
     nodes_ref, wide_ref, from_low_ref, from_high_ref, ref_ref, x_low_ref, x_high_ref,
-    wy_ref, wx_ref, out_ref, low_ref, high_ref, warp_ref, u_ref,
+    out_ref, low_ref, high_ref, warp_ref, u_ref,
 ):
     rows_wide = wide_ref.shape[1]
     size_y = rows_wide - 2 * ELEM
@@ -388,6 +443,7 @@
         return carry
 
     lax.fori_loop(0, CHUNKS, spread, 0)
+    by_y = powers(ramp((ELEM, LANES), 0), False)
 
     lane_16 = lane_of((ELEM, LANES))
     lane_8 = lane_of((8, LANES))
@@ -454,7 +510,7 @@
             for a in range(2):
                 for b in range(2):
                     total = sum(
-                        sums[half][c][a] * wy_ref[3 + b, 8 * half : 8 * half + 8, :]
+                        sums[half][c][a] * by_y[b][8 * half : 8 * half + 8, :]
                         for half in range(2)
                     )
                     kind = c * 4 + a * 2 + b
@@ -462,7 +518,7 @@
         return carry
 
     lax.fori_loop(0, count_y, row, 0)
-    out_ref[...] = contract_x(u_ref, wx_ref, out_ref.shape[0])
+    out_ref[...] = contract_x(u_ref, False, out_ref.shape[0])
 
 
 def cg_kernel(axes, gathered_ref, loads_ref, update_ref, residual_ref, m_ref, b_ref, s_ref, r_ref, d_ref):
@@ -619,21 +675,6 @@
                 out[c, a] = scale * value[: count_y + 1, : count_x + 1]
 
 
-def x_weights(count_x, weights, groups):
-    table = np.zeros((groups, LANES, LANES), np.float32)
-    for group in range(groups):
-        for u, weight in enumerate(weights):
-            for k in range(count_x):
-                column = (group * len(weights) + u) * count_x + k
-                table[group, k * ELEM : (k + 1) * ELEM, column] = weight / ELEM**2
-    return jnp.asarray(table)
-
-
-def y_weights():
-    table = np.concatenate([SQUARED, LINEAR]).astype(np.float32)
-    return jnp.asarray(np.broadcast_to(table[:, :, None], table.shape + (LANES,)))
-
-
 VMEM = pl.BlockSpec(memory_space=pltpu.VMEM)
 SMEM = pl.BlockSpec(memory_space=pltpu.SMEM)
 PARAMS = pltpu.CompilerParams(vmem_limit_bytes=48 * 2**20)
@@ -644,10 +685,10 @@
     count_y, count_x = size_y // ELEM, size_x // ELEM
     f32 = jnp.float32
     per = 8 // count_y
-    load_groups = 12 // per
     sizes = tuple(lax.axis_size(axis) for axis in ("gx", "gy", "gz"))
     groups = sizes[0] * sizes[2]
     gather_sems = pltpu.SemaphoreType.DMA((sum(sizes) - 3,))
+    direct_sems = pltpu.SemaphoreType.DMA((groups * sizes[1] - 1,))
     moments = jax.ShapeDtypeStruct(sizes + (GROUP * count_y, LANES), f32)
     wide = jax.ShapeDtypeStruct((3 * ELEM, size_y + 2 * ELEM, LANES), f32)
     face = jax.ShapeDtypeStruct((CHUNKS, size_y + 2 * ELEM, LANES), f32)
@@ -655,11 +696,10 @@
     padded = jax.ShapeDtypeStruct((size_z + 2, size_y + 16, LANES), f32)
     plane = pltpu.VMEM((size_y, LANES), f32)
     edge = pltpu.VMEM((size_z, 8, LANES), f32)
-    by_y = y_weights()
     *halos, gathered = pl.pallas_call(
         halo_kernel,
         out_shape=(wide, face, face, padded, ref_face, ref_face, moments),
-        in_specs=[VMEM] * 4,
+        in_specs=[VMEM] * 2,
         out_specs=[VMEM] * 7,
         scratch_shapes=[
             pltpu.VMEM(face.shape, f32),
@@ -679,11 +719,11 @@
         compiler_params=pltpu.CompilerParams(
             vmem_limit_bytes=48 * 2**20, collective_id=0, has_side_effects=True
         ),
-    )(ref_image, deformed_image, by_y, x_weights(count_x, SQUARED, GROUPS))
+    )(ref_image, deformed_image)
     block = pl.pallas_call(
         element_kernel,
         out_shape=jax.ShapeDtypeStruct((8, LANES), f32),
-        in_specs=[SMEM] + [VMEM] * 8,
+        in_specs=[SMEM] + [VMEM] * 6,
         out_specs=VMEM,
         scratch_shapes=[
             pltpu.VMEM(wide.shape, f32),
@@ -692,13 +732,13 @@
             pltpu.VMEM((12 * count_y, LANES), f32),
         ],
         compiler_params=PARAMS,
-    )(nodal_disp, *halos, by_y, x_weights(count_x, LINEAR, load_groups))
+    )(nodal_disp, *halos)
     loads = pl.pallas_call(
         gather_kernel,
         out_shape=jax.ShapeDtypeStruct(sizes + block.shape, f32),
         in_specs=[VMEM],
         out_specs=VMEM,
-        scratch_shapes=[gather_sems, gather_sems],
+        scratch_shapes=[direct_sems, direct_sems],
         compiler_params=pltpu.CompilerParams(
             vmem_limit_bytes=48 * 2**20, collective_id=1, has_side_effects=True
         ),

time: 67 us -> 61.6 us (0.919)
  local copies, waits for them, and re-layouts: 6.76 us -> 4.01 us
  Pallas kernels: 59.2 us -> 56.7 us
    pallas_call x1, Pallas kernels: 12.2 us -> 9.66 us  [per_device(): pl.pallas_call(gather_kernel, out_shape=jax.ShapeDtypeStruct(sizes + bloc...]
    unnamed x9 -> x5, local copies, waits for them, and re-layouts: 4.78 us -> 2.8 us
    another operation x1 -> x0, local copies, waits for them, and re-layouts: 0.76 us -> none
where the time goes in v4:
time: 61.6 us; the launch traced here: 61.4 us
  Pallas kernels  56.7 us (92%)
  local copies, waits for them, and re-layouts  4.01 us (7%)
  between operations  0.66 us (1%)
    pallas_call x1, Pallas kernels, per_device(): pl.pallas_call(halo_kernel, out_shape=(wide, face, face, padded, ref_face...  31.3 us
    pallas_call x1, Pallas kernels, per_device(): pl.pallas_call(gather_kernel, out_shape=jax.ShapeDtypeStruct(sizes + bloc...  9.66 us
    pallas_call x1, Pallas kernels, per_device(): pl.pallas_call(element_kernel, out_shape=jax.ShapeDtypeStruct((8, LANES),...  8.91 us
    pallas_call x1, Pallas kernels, per_device(): pl.pallas_call(functools.partial(cg_kernel, (count_x, count_y)), out_shap...  6.9 us
    unnamed x5, local copies, waits for them, and re-layouts  2.8 us

profile of v4, /device:TPU:0, one launch (start us, length us, event | category | flops | bytes accessed | tf_op | source)
XLA Modules:
  0.0 61.4 jit_solution(8228301162395603311)
XLA Ops:
  0.6 0.0 copy-start
  0.6 1.0 %copy-done = f32[16,64,128]{2,1,0:T(8,128)S(1)} copy-done((f32[16,64,128]{2,1,0:T(8,128)S(1)}, f32[16,64,128]{2,1,0:T(8,128)}, u32[]{:S(2)}) %copy-start) | copy-done | bytes 524312
  1.7 0.0 copy-start.1
  1.7 1.0 %copy-done.1 = f32[16,64,128]{2,1,0:T(8,128)S(1)} copy-done((f32[16,64,128]{2,1,0:T(8,128)S(1)}, f32[16,64,128]{2,1,0:T(8,128)}, u32[]{:S(2)}) %copy-start.1) | copy-done | bytes 524312
  2.7 31.3 %shard_map.50 = (f32[48,96,128]{2,1,0:T(8,128)S(1)}, f32[6,96,128]{2,1,0:T(8,128)S(1)}, f32[6,96,128]{2,1,0:T(8,128)S(1)}, f32[18,80,128]{2,1,0:T(8,128)S(1)}, f...) custom-call(f32[16,64,128]{2,1,0:T(8,128)S(1)} %copy-done, ...), custom_call_target="tpu_custom_call" | custom-call | tf_op jit(solution)/shard_map/pallas_call | solution.py:699
  34.0 0.7 %copy.5.nodes_ref = s32[3,2,5,9]{3,2,1,0:T(8,128)S(1)} copy(s32[3,2,5,9]{3,1,2,0:T(2,128)} %param.5) | data formatting | bytes 2160 | tf_op args[2]
  34.7 8.9 %shard_map.51.block_ref = f32[8,128]{1,0:T(8,128)S(1)} custom-call(s32[3,2,5,9]{3,2,1,0:T(8,128)S(1)} %copy.5.nodes_ref, f32[48,96,128]{2,1,0:T(8,128)S(1)} %get-tuple-element.10.wide_ref, f32[6,96,128]{2,1,0:T(8,128)S(1)} %get-tuple-element.11.from_low_ref, f32[6,96,128]{2,1,0:T(8,128)S(1)} %get-tuple-element.12.from_high_ref, ...), custom_call_target="tpu_custom_call" | custom-call | tf_op jit(solution)/shard_map/pallas_call | solution.py:723
  43.6 9.7 %shard_map.52.loads_ref = f32[4,2,4,8,128]{4,3,2,1,0:T(8,128)S(1)} custom-call(f32[8,128]{1,0:T(8,128)S(1)} %shard_map.51.block_ref), custom_call_target="tpu_custom_call" | custom-call | tf_op jit(solution)/shard_map/pallas_call | solution.py:736
  53.3 6.9 %shard_map.53 = (f32[3,2,5,9]{3,2,1,0:T(8,128)S(1)}, f32[3,2,5,9]{3,2,1,0:T(8,128)S(1)}) custom-call(f32[4,2,4,48,128]{4,3,2,1,0:T(8,128)S(1)} %get-tuple-element.9.gathered_ref, f32[4,2,4,8,128]{4,3,2,1,0:T(8,128)S(1)} %shard_map.52.loads_ref), custom_call_target="tpu_custom_call" | custom-call | tf_op jit(solution)/shard_map/pallas_call | solution.py:749
  60.2 0.6 copy.6
  60.8 0.6 copy.7
Async XLA Ops:
  0.6 1.0 %copy-start = (f32[16,64,128]{2,1,0:T(8,128)S(1)}, f32[16,64,128]{2,1,0:T(8,128)}, u32[]{:S(2)}) copy-start(f32[16,64,128]{2,1,0:T(8,128)} %image_ref.1) | copy-start | bytes 1572868
  1.7 1.0 %copy-start.1 = (f32[16,64,128]{2,1,0:T(8,128)S(1)}, f32[16,64,128]{2,1,0:T(8,128)}, u32[]{:S(2)}) copy-start(f32[16,64,128]{2,1,0:T(8,128)} %deformed_ref.1) | copy-start | bytes 1572868

commit v5 on v4

--- a/solution.py
+++ b/solution.py
@@ -101,6 +101,21 @@
         for own in self.held:
             self.send(self.ref.at[own], self.ref.at[flip(own, step)], self.x_peers[number])
         self.held = self.held + [flip(own, step) for own in self.held]
+
+    def run_x(self):
+        arrivals = [[] for _ in self.steps]
+
+        def push(own, first):
+            for number in range(first, len(self.steps)):
+                other = flip(own, self.steps[number])
+                self.send(self.ref.at[own], self.ref.at[other], self.x_peers[number])
+                arrivals[number].append((self.phase.pop(), other))
+
+        push(self.at[0], 0)
+        for number in range(len(self.steps)):
+            for copy, block in arrivals[number]:
+                copy.wait_recv()
+                push(block, number + 1)
 
     def finish(self):
         for copy in self.sent:
@@ -363,9 +378,7 @@
     for chunk, arrivals in late:
         x_faces((chunk,), arrivals)
     gather.arrive()
-    for number in range(len(gather.steps)):
-        gather.start_x(number)
-        gather.arrive()
+    gather.run_x()
     for arrive in final:
         arrive()
     gather.finish()

time: 61.6 us -> 61.4 us (level)
  no operation moved by 1% of the time
where the time goes in v5:
time: 61.4 us; the launch traced here: 61.1 us
  Pallas kernels  56.4 us (92%)
  local copies, waits for them, and re-layouts  4.01 us (7%)
  between operations  0.66 us (1%)
    pallas_call x1, Pallas kernels, per_device(): pl.pallas_call(halo_kernel, out_shape=(wide, face, face, padded, ref_face...  31 us
    pallas_call x1, Pallas kernels, per_device(): pl.pallas_call(gather_kernel, out_shape=jax.ShapeDtypeStruct(sizes + bloc...  9.66 us
    pallas_call x1, Pallas kernels, per_device(): pl.pallas_call(element_kernel, out_shape=jax.ShapeDtypeStruct((8, LANES),...  8.91 us
    pallas_call x1, Pallas kernels, per_device(): pl.pallas_call(functools.partial(cg_kernel, (count_x, count_y)), out_shap...  6.9 us
    unnamed x5, local copies, waits for them, and re-layouts  2.8 us

profile of v5, /device:TPU:0, one launch (start us, length us, event | category | flops | bytes accessed | tf_op | source)
XLA Modules:
  0.0 61.1 jit_solution(8556171343820205090)
XLA Ops:
  0.6 0.0 copy-start
  0.6 1.0 %copy-done = f32[16,64,128]{2,1,0:T(8,128)S(1)} copy-done((f32[16,64,128]{2,1,0:T(8,128)S(1)}, f32[16,64,128]{2,1,0:T(8,128)}, u32[]{:S(2)}) %copy-start) | copy-done | bytes 524312
  1.7 0.0 copy-start.1
  1.7 1.0 %copy-done.1 = f32[16,64,128]{2,1,0:T(8,128)S(1)} copy-done((f32[16,64,128]{2,1,0:T(8,128)S(1)}, f32[16,64,128]{2,1,0:T(8,128)}, u32[]{:S(2)}) %copy-start.1) | copy-done | bytes 524312
  2.7 31.0 %shard_map.50 = (f32[48,96,128]{2,1,0:T(8,128)S(1)}, f32[6,96,128]{2,1,0:T(8,128)S(1)}, f32[6,96,128]{2,1,0:T(8,128)S(1)}, f32[18,80,128]{2,1,0:T(8,128)S(1)}, f...) custom-call(f32[16,64,128]{2,1,0:T(8,128)S(1)} %copy-done, ...), custom_call_target="tpu_custom_call" | custom-call | tf_op jit(solution)/shard_map/pallas_call | solution.py:712
  33.7 0.7 %copy.5.nodes_ref = s32[3,2,5,9]{3,2,1,0:T(8,128)S(1)} copy(s32[3,2,5,9]{3,1,2,0:T(2,128)} %param.5) | data formatting | bytes 2160 | tf_op args[2]
  34.4 8.9 %shard_map.51.block_ref = f32[8,128]{1,0:T(8,128)S(1)} custom-call(s32[3,2,5,9]{3,2,1,0:T(8,128)S(1)} %copy.5.nodes_ref, f32[48,96,128]{2,1,0:T(8,128)S(1)} %get-tuple-element.10.wide_ref, f32[6,96,128]{2,1,0:T(8,128)S(1)} %get-tuple-element.11.from_low_ref, f32[6,96,128]{2,1,0:T(8,128)S(1)} %get-tuple-element.12.from_high_ref, ...), custom_call_target="tpu_custom_call" | custom-call | tf_op jit(solution)/shard_map/pallas_call | solution.py:736
  43.3 9.7 %shard_map.52.loads_ref = f32[4,2,4,8,128]{4,3,2,1,0:T(8,128)S(1)} custom-call(f32[8,128]{1,0:T(8,128)S(1)} %shard_map.51.block_ref), custom_call_target="tpu_custom_call" | custom-call | tf_op jit(solution)/shard_map/pallas_call | solution.py:749
  53.0 6.9 %shard_map.53 = (f32[3,2,5,9]{3,2,1,0:T(8,128)S(1)}, f32[3,2,5,9]{3,2,1,0:T(8,128)S(1)}) custom-call(f32[4,2,4,48,128]{4,3,2,1,0:T(8,128)S(1)} %get-tuple-element.9.gathered_ref, f32[4,2,4,8,128]{4,3,2,1,0:T(8,128)S(1)} %shard_map.52.loads_ref), custom_call_target="tpu_custom_call" | custom-call | tf_op jit(solution)/shard_map/pallas_call | solution.py:762
  59.9 0.6 copy.6
  60.5 0.6 copy.7
Async XLA Ops:
  0.6 1.0 %copy-start = (f32[16,64,128]{2,1,0:T(8,128)S(1)}, f32[16,64,128]{2,1,0:T(8,128)}, u32[]{:S(2)}) copy-start(f32[16,64,128]{2,1,0:T(8,128)} %image_ref.1) | copy-start | bytes 1572868
  1.7 1.0 %copy-start.1 = (f32[16,64,128]{2,1,0:T(8,128)S(1)}, f32[16,64,128]{2,1,0:T(8,128)}, u32[]{:S(2)}) copy-start(f32[16,64,128]{2,1,0:T(8,128)} %deformed_ref.1) | copy-start | bytes 1572868
